TPU v7x, 32 devices: a whole 2x2x4 slice. The times are simulated.
32 devices in a mesh: batch: 4 (over y, x), wide: 8 (over z, core).
Axes of the slice: x: 2, y: 2, z: 4, core: 2. Of those that a mesh axis runs over, the one named last changes fastest.
Arguments:
- block_in: bfloat16 [16, 512, 384], P('batch', 'wide'), may hold values from -6 to 6
- lead_embed: bfloat16 [16, 384], P('batch'), may hold values from -6 to 6
- lengths: int32 [16], P('batch'), may hold values from 128 to 512, as said below
- w_ada: bfloat16 [384, 2304], replicated, may hold values from -0.3125 to 0.3125
- b_ada: bfloat16 [2304], replicated, may hold values from -3 to 3
- w_qkv: bfloat16 [384, 1152], replicated, may hold values from -0.3125 to 0.3125
- w_proj: bfloat16 [384, 384], replicated, may hold values from -1.25 to 1.25
- w_fc1: bfloat16 [384, 1536], replicated, may hold values from -0.3125 to 0.3125
- w_fc2: bfloat16 [1536, 384], replicated, may hold values from -0.15625 to 0.15625
- cotangent: bfloat16 [16, 512, 384], P('batch', 'wide'), may hold values from -6 to 6
Outputs:
- block_out: float32 [16, 512, 384], P('batch', 'wide')
- input_grad: float32 [16, 512, 384], P('batch', 'wide')
- ada_grad: float32 [384, 2304], replicated
- bias_grad: float32 [2304], replicated
- qkv_grad: float32 [384, 1152], replicated
- proj_grad: float32 [384, 384], replicated
- fc1_grad: float32 [384, 1536], replicated
- fc2_grad: float32 [1536, 384], replicated
Inputs may be any that keep to these rules, and one draw needn't show every extreme that they name: `lengths`: each batch group of 4 items has max(1, 0) items of exactly 512 patches, which ones drawn at random; the others have 512 // 4 to 384.
All inputs are finite; a program needn't handle non-finite values.
Results may differ from a plain program's by a relative error of at most 0.012.
The roundings to bfloat16 on the way count: a program that leaves them out, or rounds other values in their place, can miss the bound.
Values may be sent and summed in bfloat16 or wider, within the bound.
A program may use at most 512 MiB of HBM per device.

v0:
```python
from functools import partial

import jax
import jax.numpy as jnp
from jax import lax
from jax.sharding import PartitionSpec as P

HEADS = 6
HEAD_DIM = 64


EPS = 1e-06


def norm_rows(values):
    center = values - jnp.mean(values, axis=-1, keepdims=True)
    inverse = lax.rsqrt(jnp.mean(center * center, axis=-1, keepdims=True) + EPS)
    return (center * inverse, inverse)


def norm_back(normed, inverse, gradient):
    return inverse * (
        gradient
        - jnp.mean(gradient, axis=-1, keepdims=True)
        - normed * jnp.mean(gradient * normed, axis=-1, keepdims=True)
    )


def to_heads(tokens, part_count, head_count, head_size):
    item_count, span_len, _ = tokens.shape
    shaped = tokens.reshape(item_count, span_len, part_count, head_count, head_size)
    return shaped.transpose(2, 0, 3, 1, 4).reshape(
        part_count, item_count * head_count, span_len * head_size
    )


def from_heads(blocks, item_count, head_count, head_size):
    part_count = blocks.shape[0]
    span_len = blocks.shape[2] // head_size
    shaped = blocks.reshape(part_count, item_count, head_count, span_len, head_size)
    return shaped.transpose(1, 3, 0, 2, 4).reshape(
        item_count, span_len, part_count * head_count * head_size
    )


def split_rows(values, block_rows):
    pair_count, slot_len = (values.shape[0], values.shape[1])
    rest = values.shape[2:]
    shaped = values.reshape((pair_count, slot_len // block_rows, block_rows) + rest)
    return jnp.moveaxis(shaped, 1, 0)


def join_rows(values):
    merged = jnp.moveaxis(values, 0, 1)
    return merged.reshape((merged.shape[0], merged.shape[1] * merged.shape[2]) + merged.shape[3:])


def masked_scores(query_block, keys_all, key_valid, inv_root):
    scores = (
        jnp.einsum("pqd,pkd->pqk", query_block, keys_all, preferred_element_type=jnp.float32)
        * inv_root
    )
    return jnp.where(key_valid[:, None, :], scores, -1e30)


def attend_forward(queries, keys_all, values, key_valid, inv_root):
    block_rows = min(512, queries.shape[1])

    def one_block(query_block):
        scores = masked_scores(query_block, keys_all, key_valid, inv_root)
        row_peak = jnp.max(scores, axis=-1, keepdims=True)
        exp_scores = jnp.exp(scores - row_peak)
        row_total = jnp.sum(exp_scores, axis=-1, keepdims=True)
        weights = (exp_scores / row_total).astype(jnp.bfloat16)
        outcome = jnp.einsum("pqk,pkd->pqd", weights, values, preferred_element_type=jnp.float32)
        return (outcome.astype(jnp.bfloat16), (row_peak + jnp.log(row_total))[..., 0])

    outputs, logsum = lax.map(one_block, split_rows(queries, block_rows))
    return (join_rows(outputs), join_rows(logsum))


def attend_backward(queries, keys_all, values, out_grad, logsum, key_valid, inv_root):
    block_rows = min(512, queries.shape[1])
    zeros = jnp.zeros(keys_all.shape, jnp.float32)

    def one_block(carried, packed):
        key_grad, value_grad = carried
        query_block, grad_block, logsum_block = packed
        scores = masked_scores(query_block, keys_all, key_valid, inv_root)
        weights = jnp.exp(scores - logsum_block[..., None])
        weight_grad = jnp.einsum(
            "pqd,pkd->pqk", grad_block, values, preferred_element_type=jnp.float32
        )
        score_grad = weights * (
            weight_grad - jnp.sum(weights * weight_grad, axis=-1, keepdims=True)
        )
        score_grad = score_grad.astype(jnp.bfloat16)
        query_grad = (
            jnp.einsum("pqk,pkd->pqd", score_grad, keys_all, preferred_element_type=jnp.float32)
            * inv_root
        )
        key_grad = (
            key_grad
            + jnp.einsum(
                "pqk,pqd->pkd", score_grad, query_block, preferred_element_type=jnp.float32
            )
            * inv_root
        )
        value_grad = value_grad + jnp.einsum(
            "pqk,pqd->pkd",
            weights.astype(jnp.bfloat16),
            grad_block,
            preferred_element_type=jnp.float32,
        )
        return ((key_grad, value_grad), query_grad)

    packed = (
        split_rows(queries, block_rows),
        split_rows(out_grad, block_rows),
        split_rows(logsum, block_rows),
    )
    (key_grad, value_grad), query_grads = lax.scan(one_block, (zeros, zeros), packed)
    return jnp.stack([join_rows(query_grads), key_grad, value_grad]).astype(jnp.bfloat16)


def on_device(block_in, lead_embed, lengths, w_ada, b_ada, w_qkv, w_proj, w_fc1, w_fc2, cotangent):
    item_count, span_len, width = block_in.shape
    head_count = HEADS
    head_size = HEAD_DIM
    shards = lax.axis_size("wide")
    pair_count = item_count * head_count // shards
    slot_len = span_len * shards
    inv_root = HEAD_DIM ** (-0.5)
    inputs = block_in.astype(jnp.float32)
    condition = jax.nn.silu(lead_embed.astype(jnp.float32)).astype(jnp.bfloat16)
    modulation = jnp.dot(condition, w_ada, preferred_element_type=jnp.float32) + b_ada.astype(
        jnp.float32
    )
    pieces = [modulation[:, None, column * width : (column + 1) * width] for column in range(6)]
    shift_att, scale_att, gate_att, shift_mlp, scale_mlp, gate_mlp = pieces
    normed, norm_inverse = norm_rows(inputs)
    entry = (normed * (1.0 + scale_att) + shift_att).astype(jnp.bfloat16)
    triple = jnp.dot(entry, w_qkv, preferred_element_type=jnp.float32).astype(jnp.bfloat16)
    arrived = lax.all_to_all(
        to_heads(triple, 3, head_count, head_size), "wide", split_axis=1, concat_axis=2, tiled=True
    )
    heads_in = arrived.reshape(3, pair_count, slot_len, head_size)
    pair_ids = lax.axis_index("wide") * pair_count + jnp.arange(pair_count, dtype=jnp.int32)
    item_ids = pair_ids // head_count
    pair_length = jnp.sum(
        jnp.where(
            jnp.arange(item_count, dtype=jnp.int32)[None, :] == item_ids[:, None],
            lengths[None, :],
            0,
        ),
        axis=1,
    )
    key_valid = jnp.arange(slot_len, dtype=jnp.int32)[None, :] < pair_length[:, None]
    mixed_heads, logsum = attend_forward(heads_in[0], heads_in[1], heads_in[2], key_valid, inv_root)
    returned = lax.all_to_all(
        mixed_heads.reshape(pair_count, slot_len * head_size),
        "wide",
        split_axis=1,
        concat_axis=0,
        tiled=True,
    )
    mixed_tok = from_heads(returned[None], item_count, head_count, head_size)
    branch = jnp.dot(mixed_tok, w_proj, preferred_element_type=jnp.float32)
    middle = inputs + gate_att * branch
    second_normed, second_inverse = norm_rows(middle)
    second = (second_normed * (1.0 + scale_mlp) + shift_mlp).astype(jnp.bfloat16)
    hidden = jnp.dot(second, w_fc1, preferred_element_type=jnp.float32)
    active = jax.nn.gelu(hidden, approximate=False).astype(jnp.bfloat16)
    mlp_out = jnp.dot(active, w_fc2, preferred_element_type=jnp.float32)
    block_out = middle + gate_mlp * mlp_out
    gradient = cotangent.astype(jnp.float32)
    mlp_grad = (gate_mlp * gradient).astype(jnp.bfloat16)
    gate_mlp_grad = jnp.sum(gradient * mlp_out, axis=1)
    fc2_grad = jnp.einsum("isf,isd->fd", active, mlp_grad, preferred_element_type=jnp.float32)
    active_grad = jnp.dot(mlp_grad, w_fc2.T, preferred_element_type=jnp.float32)
    hidden_grad = jax.vjp(partial(jax.nn.gelu, approximate=False), hidden)[1](active_grad)[0]
    hidden_grad = hidden_grad.astype(jnp.bfloat16)
    fc1_grad = jnp.einsum("isd,isf->df", second, hidden_grad, preferred_element_type=jnp.float32)
    second_grad = jnp.dot(hidden_grad, w_fc1.T, preferred_element_type=jnp.float32)
    scale_mlp_grad = jnp.sum(second_grad * second_normed, axis=1)
    shift_mlp_grad = jnp.sum(second_grad, axis=1)
    middle_grad = gradient + norm_back(
        second_normed, second_inverse, second_grad * (1.0 + scale_mlp)
    )
    branch_grad = (gate_att * middle_grad).astype(jnp.bfloat16)
    gate_att_grad = jnp.sum(middle_grad * branch, axis=1)
    proj_grad = jnp.einsum(
        "isd,ise->de", mixed_tok, branch_grad, preferred_element_type=jnp.float32
    )
    mixed_grad = jnp.dot(branch_grad, w_proj.T, preferred_element_type=jnp.float32).astype(
        jnp.bfloat16
    )
    heads_grad = lax.all_to_all(
        to_heads(mixed_grad, 1, head_count, head_size)[0],
        "wide",
        split_axis=0,
        concat_axis=1,
        tiled=True,
    )
    heads_grad = heads_grad.reshape(pair_count, slot_len, head_size)
    again_in, _ = lax.optimization_barrier((inputs, heads_grad))
    again_normed, _ = norm_rows(again_in)
    again_entry = (again_normed * (1.0 + scale_att) + shift_att).astype(jnp.bfloat16)
    again_triple = jnp.dot(again_entry, w_qkv, preferred_element_type=jnp.float32).astype(
        jnp.bfloat16
    )
    again_heads = lax.all_to_all(
        to_heads(again_triple, 3, head_count, head_size),
        "wide",
        split_axis=1,
        concat_axis=2,
        tiled=True,
    )
    used_heads = again_heads.reshape(3, pair_count, slot_len, head_size)
    triple_grad = attend_backward(
        used_heads[0], used_heads[1], used_heads[2], heads_grad, logsum, key_valid, inv_root
    )
    sent_back = lax.all_to_all(
        triple_grad.reshape(3, pair_count, slot_len * head_size),
        "wide",
        split_axis=2,
        concat_axis=1,
        tiled=True,
    )
    token_grad = from_heads(sent_back, item_count, head_count, head_size)
    qkv_grad = jnp.einsum("isd,ise->de", entry, token_grad, preferred_element_type=jnp.float32)
    entry_grad = jnp.dot(token_grad, w_qkv.T, preferred_element_type=jnp.float32)
    scale_att_grad = jnp.sum(entry_grad * normed, axis=1)
    shift_att_grad = jnp.sum(entry_grad, axis=1)
    input_grad = middle_grad + norm_back(normed, norm_inverse, entry_grad * (1.0 + scale_att))
    modulation_grad = jnp.concatenate(
        [
            shift_att_grad,
            scale_att_grad,
            gate_att_grad,
            shift_mlp_grad,
            scale_mlp_grad,
            gate_mlp_grad,
        ],
        axis=-1,
    )
    ada_grad = jnp.dot(
        condition.astype(jnp.float32).T, modulation_grad, precision=lax.Precision.HIGHEST
    )
    bias_grad = jnp.sum(modulation_grad, axis=0)
    totals = lax.psum(
        (ada_grad, bias_grad, qkv_grad, proj_grad, fc1_grad, fc2_grad), ("batch", "wide")
    )
    return (block_out, input_grad, totals[0], totals[1], totals[2], totals[3], totals[4], totals[5])


def solution(mesh):
    return jax.shard_map(
        on_device,
        mesh=mesh,
        in_specs=(
            P("batch", "wide", None),
            P("batch", None),
            P("batch"),
            P(),
            P(),
            P(),
            P(),
            P(),
            P(),
            P("batch", "wide", None),
        ),
        out_specs=(
            P("batch", "wide", None),
            P("batch", "wide", None),
            P(),
            P(),
            P(),
            P(),
            P(),
            P(),
        ),
        check_vma=False,
    )
```

profile of v0, /device:TPU:0, one launch (start us, length us, event | category | flops | bytes accessed | tf_op | source)
XLA Modules:
  0.0 529.1 jit_solution(15474611542126083640)
XLA Ops:
  14.2 6.5 %all-to-all-start = ((bf16[3,24,4096]{2,0,1:T(4,128)(2,1)}), bf16[3,24,4096]{2,0,1:T(4,128)(2,1)}, u32[]{:S(2)}, u32[]{:S(2)}) async-start(bf16[3,24,4096]{2,0,1:T(4,128)(2,1)} %reshape.204), calls=%async_computation | async-start | bytes 1572864 | tf_op jit(solution)/shard_map/all_to_all | solution.py:144
  24.8 16.9 %all-to-all-done = bf16[3,24,4096]{2,0,1:T(4,128)(2,1)} async-done(((bf16[3,24,4096]{2,0,1:T(4,128)(2,1)}), bf16[3,24,4096]{2,0,1:T(4,128)(2,1)}, u32[]{:S(2)}, u32[]{:S(2)}) %all-to-all-start) | async-done | bytes 589856 | tf_op jit(solution)/shard_map/all_to_all | solution.py:144
  41.7 3.5 all-to-all-start.2
  48.4 2.3 fusion
  51.2 2.4 fusion.1
  56.5 9.6 %all-to-all-done.2 = bf16[3,24,4096]{2,0,1:T(4,128)(2,1)S(1)} async-done(((bf16[3,24,4096]{2,0,1:T(4,128)(2,1)}), bf16[3,24,4096]{2,0,1:T(4,128)(2,1)S(1)}, u32[]{:S(2)}, u32[]{:S(2)}) %all-to-all-start.2) | async-done | bytes 589856 | tf_op jit(solution)/shard_map/all_to_all | solution.py:212
  66.2 3.6 all-to-all-start.1
  70.4 9.0 %all-to-all-done.1 = bf16[3,8,4096]{2,0,1:T(4,128)(2,1)S(1)} async-done(((bf16[3,8,4096]{2,0,1:T(4,128)(2,1)}), bf16[3,8,4096]{2,0,1:T(4,128)(2,1)S(1)}, u32[]{:S(2)}, u32[]{:S(2)}) %all-to-all-start.1) | async-done | bytes 196640 | tf_op jit(solution)/shard_map/all_to_all | solution.py:160
  81.1 2.2 fusion.31
  83.3 3.6 multiply_convert_fusion.1
  95.0 4.3 all-to-all-start.3
  103.5 5.4 %all-to-all-done.3 = bf16[8,3,4096]{2,1,0:T(4,128)(2,1)} async-done(((bf16[8,3,4096]{2,1,0:T(4,128)(2,1)}), bf16[8,3,4096]{2,1,0:T(4,128)(2,1)}, u32[]{:S(2)}, u32[]{:S(2)}) %all-to-all-start.3) | async-done | bytes 196640 | tf_op jit(solution)/shard_map/all_to_all | solution.py:198
  122.2 31.8 %copy.125 = bf16[3,3,32768]{1,0,2:T(4,128)(2,1)} copy(bf16[3,3,32768]{2,1,0:T(4,128)(2,1)S(1)} %pad_maximum_fusion) | data formatting | bytes 1179648 | tf_op jit(solution)/shard_map/stack | solution.py:123
  153.9 32.1 %reshape.206 = bf16[8,2,18432]{2,1,0:T(2,128)(2,1)} reshape(bf16[32768,3,3]{2,1,0:T(4,128)(2,1)} %bitcast.105) | data formatting | bytes 1179648
  186.0 3.7 all-to-all-start.4
  191.2 2.0 convolution_bitcast_fusion
  193.2 2.0 convolution_bitcast_fusion.1
  195.2 11.2 %all-to-all-done.4 = bf16[8,2,18432]{2,1,0:T(2,128)(2,1)S(1)} async-done(((bf16[8,2,18432]{2,1,0:T(2,128)(2,1)}), bf16[8,2,18432]{2,1,0:T(2,128)(2,1)S(1)}, u32[]{:S(2)}, u32[]{:S(2)}) %all-to-all-start.4) | async-done | bytes 589856 | tf_op jit(solution)/shard_map/all_to_all | solution.py:223
  206.4 33.2 %reshape.207 = bf16[32768,3,3]{2,1,0:T(4,128)(2,1)} reshape(bf16[8,2,18432]{2,1,0:T(2,128)(2,1)S(1)} %all-to-all-done.4) | data formatting | bytes 1179648
  239.6 42.2 %copy.126 = bf16[3,3,8,4096]{3,1,2,0:T(4,128)(2,1)S(1)} copy(bf16[3,3,8,4096]{1,0,3,2:T(4,128)(2,1)} %bitcast.106) | data formatting | bytes 1179648 | tf_op jit(solution)/shard_map/all_to_all | solution.py:223
  289.3 3.4 fusion.46
  292.8 39.2 %psum.43 = f32[2304]{0:T(1024)} all-reduce(f32[2304]{0:T(1024)S(1)} %reduce_sum.201), channel_id=1, replica_groups=mesh['batch'=4,'wide'=8] {'batch','wide'}, use_global_device_ids=true, to_apply=%region_22.23 | all-reduce | flops 2304 | bytes 18432 | tf_op jit(solution)/shard_map/psum | solution.py:251
  332.9 178.2 %all-reduce.3.cloned.1.call-done = (f32[384,2304]{1,0:T(8,128)}, f32[384,1152]{1,0:T(8,128)}, f32[384,384]{1,0:T(8,128)}, f32[384,1536]{1,0:T(8,128)}, f32[1536,384]{1,0:T(8,128)}) async-done(((f32[384,2304]{1,0:T(8,128)}, f32[384,1152]{1,0:T(8,128)}, f32[384,384]{1,0:T(8,128)}, f32[384,1536]{1,0:T(8,128)}, f32[1536,384]{1,0:T(8,128)}), (f32[384,2304]{1,0:T(8,128)}, f32[384,1152]{1,0:T(8,128)}, ...) | async-done | bytes 10616848 | tf_op jit(solution)/shard_map/psum | solution.py:251
  511.1 4.2 copy.162
  (200 shorter events, 61.4 us)
Async XLA Ops:
  7.2 3.1 copy-start.3
  7.2 3.5 copy-start.4
  10.3 10.7 %copy-start.21 = (f32[4,384]{1,0:T(4,128)}, f32[4,384]{1,0:T(4,128)S(1)}, u32[]{:S(2)}) copy-start(f32[4,384]{1,0:T(4,128)S(1)} %get-tuple-element.93) | copy-start | bytes 18436
  14.2 6.8 %copy-start.5 = (bf16[384,1152]{1,0:T(8,128)(2,1)S(1)}, bf16[384,1152]{1,0:T(8,128)(2,1)}, u32[]{:S(2)}) copy-start(bf16[384,1152]{1,0:T(8,128)(2,1)} %param.15) | copy-start | bytes 2654212
  14.2 27.5 %all-to-all-start = ((bf16[3,24,4096]{2,0,1:T(4,128)(2,1)}), bf16[3,24,4096]{2,0,1:T(4,128)(2,1)}, u32[]{:S(2)}, u32[]{:S(2)}) async-start(bf16[3,24,4096]{2,0,1:T(4,128)(2,1)} %reshape.204), calls=%async_computation | async-start | bytes 1572864 | tf_op jit(solution)/shard_map/all_to_all | solution.py:144
  24.8 28.9 %copy-start.28 = (pred[3,512]{1,0:T(4,128)(4,1)}, pred[3,512]{1,0:T(4,128)(4,1)S(1)}, u32[]{:S(2)}) copy-start(pred[3,512]{1,0:T(4,128)(4,1)S(1)} %iota_compare_fusion) | copy-start | bytes 4612
  41.7 24.5 %all-to-all-start.2 = ((bf16[3,24,4096]{2,0,1:T(4,128)(2,1)}), bf16[3,24,4096]{2,0,1:T(4,128)(2,1)S(1)}, u32[]{:S(2)}, u32[]{:S(2)}) async-start(bf16[3,24,4096]{2,0,1:T(4,128)(2,1)} %reshape.205), calls=%async_computation.2 | async-start | bytes 1572864 | tf_op jit(solution)/shard_map/all_to_all | solution.py:212
  50.7 3.0 copy-start.19
  66.2 13.2 %all-to-all-start.1 = ((bf16[3,8,4096]{2,0,1:T(4,128)(2,1)}), bf16[3,8,4096]{2,0,1:T(4,128)(2,1)S(1)}, u32[]{:S(2)}, u32[]{:S(2)}) async-start(bf16[3,8,4096]{2,0,1:T(4,128)(2,1)} %copy.102), calls=%async_computation.1 | async-start | bytes 524288 | tf_op jit(solution)/shard_map/all_to_all | solution.py:160
  69.8 10.7 %copy-start.12 = (bf16[384,384]{1,0:T(8,128)(2,1)S(1)}, bf16[384,384]{1,0:T(8,128)(2,1)}, u32[]{:S(2)}) copy-start(bf16[384,384]{1,0:T(8,128)(2,1)} %param.16) | copy-start | bytes 884740
  80.8 8.6 %copy-start.39 = (f32[4,64]{1,0:T(4,128)}, f32[4,64]{1,0:T(4,128)S(1)}, u32[]{:S(2)}) copy-start(f32[4,64]{1,0:T(4,128)S(1)} %broadcast_multiply_fusion.5) | copy-start | bytes 3076
  81.0 8.4 %copy-start.42 = (f32[4,64]{1,0:T(4,128)}, f32[4,64]{1,0:T(4,128)S(1)}, u32[]{:S(2)}) copy-start(f32[4,64]{1,0:T(4,128)S(1)} %add_rsqrt_fusion.1) | copy-start | bytes 3076
  83.2 3.6 copy-start.13
  83.3 3.6 copy-start.17
  83.3 3.6 copy-start.33
  88.2 3.2 copy-start.50
  95.0 14.0 %all-to-all-start.3 = ((bf16[8,3,4096]{2,1,0:T(4,128)(2,1)}), bf16[8,3,4096]{2,1,0:T(4,128)(2,1)}, u32[]{:S(2)}, u32[]{:S(2)}) async-start(bf16[8,3,4096]{2,1,0:T(4,128)(2,1)} %all_to_all.66), calls=%async_computation.3 | async-start | bytes 524288 | tf_op jit(solution)/shard_map/all_to_all | solution.py:198
  102.9 9.8 %copy-start.7 = (bf16[3,512,64]{2,1,0:T(8,128)(2,1)}, bf16[3,512,64]{2,1,0:T(8,128)(2,1)S(1)}, u32[]{:S(2)}) copy-start(bf16[3,512,64]{2,1,0:T(8,128)(2,1)S(1)} %squeeze.34) | copy-start | bytes 589828
  186.0 5.1 copy-start.18
  186.0 5.1 copy-start.34
  186.0 20.4 %all-to-all-start.4 = ((bf16[8,2,18432]{2,1,0:T(2,128)(2,1)}), bf16[8,2,18432]{2,1,0:T(2,128)(2,1)S(1)}, u32[]{:S(2)}, u32[]{:S(2)}) async-start(bf16[8,2,18432]{2,1,0:T(2,128)(2,1)} %reshape.206), calls=%async_computation.4 | async-start | bytes 1179648 | tf_op jit(solution)/shard_map/all_to_all | solution.py:223
  189.7 321.4 %all-reduce.3.cloned.1.call-start = ((), (), s32[]{:S(2)}) async-start(), calls=%async_computation.5 | async-start | bytes 21233664 | tf_op jit(solution)/shard_map/psum | solution.py:251
  511.1 4.2 copy-start.11
  517.9 3.9 copy-start.1
  (34 other events, 58.7 us)
Sparse Core Ops, SparseCore 0:
  292.9 218.1 all-reduce.2
where the time goes:
time: 538 us; the launch traced here: 529 us
  waiting for transfers between devices  230 us (43%)
  local copies, waits for them, and re-layouts  181 us (34%)
  blocking collectives  39.2 us (7%)
  matrix products  28.7 us (5%)
  starting transfers between devices  21.8 us (4%)
  between operations  15.4 us (3%)
  other arithmetic  12.8 us (2%)
    psum x1, waiting for transfers between devices, on_device(): lax.psum((ada_grad, bias_grad, qkv_grad, proj_grad, fc1_grad, fc2_grad),...  178 us
    unnamed x116, local copies, waits for them, and re-layouts  77.8 us
    all_to_all x1, local copies, waits for them, and re-layouts, on_device(): lax.all_to_all(triple_grad.reshape(3, pair_count, slot_len * head_size),...  42.2 us
    psum x1, blocking collectives, on_device(): lax.psum((ada_grad, bias_grad, qkv_grad, proj_grad, fc1_grad, fc2_grad),...  39.2 us
    another operation x4, local copies, waits for them, and re-layouts, attend_backward(): jnp.stack([join_rows(query_grads), key_grad, value_grad])  34.2 us
    all_to_all x1, waiting for transfers between devices, on_device(): lax.all_to_all(to_heads(triple, 3, head_count, head_size), 'wide', split_...  16.9 us
    all_to_all x1, waiting for transfers between devices, on_device(): lax.all_to_all(triple_grad.reshape(3, pair_count, slot_len * head_size),...  11.2 us
  transfers between devices with their start and end apart: 6, of which 6 were waited for; matrix products, arithmetic and copies ran while one was open for 5% of the time, Pallas kernels for 0%

commit v1 on v0

--- a/solution.py
+++ b/solution.py
@@ -1,8 +1,11 @@
+import math
 from functools import partial
 
 import jax
 import jax.numpy as jnp
 from jax import lax
+from jax.experimental import pallas as pl
+from jax.experimental.pallas import tpu as pltpu
 from jax.sharding import PartitionSpec as P
 
 HEADS = 6
@@ -254,9 +257,673 @@
     return (block_out, input_grad, totals[0], totals[1], totals[2], totals[3], totals[4], totals[5])
 
 
+MESH = pl.DeviceIdType.MESH
+MM = (((1,), (0,)), ((), ()))
+NT = (((1,), (1,)), ((), ()))
+TN = (((0,), (0,)), ((), ()))
+B16 = jnp.bfloat16
+F32 = jnp.float32
+
+
+def dot(left, right, dims):
+    return lax.dot_general(left, right, dims, preferred_element_type=F32)
+
+
+def col_sum(values):
+    return jnp.sum(values, axis=0, keepdims=True)
+
+
+def fused_kernel(
+    lengths,
+    block_in,
+    cotangent,
+    lead_embed,
+    b_ada,
+    w_ada_in,
+    w_qkv_in,
+    w_proj_in,
+    w_fc1_in,
+    w_fc2_in,
+    out_block,
+    out_input,
+    out_fc2,
+    out_fc1,
+    out_qkvp,
+    out_mod,
+    w_ada,
+    w_qkv,
+    w_proj,
+    w_fc1,
+    w_fc2,
+    xall,
+    gall,
+    mod_rows,
+    entry,
+    normed_own,
+    q_all,
+    kv_all,
+    bias_keys,
+    probs,
+    mixed,
+    middle_ref,
+    active,
+    gelu_slope,
+    hidden_grad,
+    grads_bf,
+    send_out,
+    entry_send,
+    entry_recv,
+    qkvp,
+    core_out,
+    core_in,
+    hold,
+    stage1,
+    stage1_in,
+    stage2,
+    stage2_in,
+    stage3,
+    stage3_in,
+    stage4,
+    stage4_in,
+    total,
+    mod_own,
+    mod_in,
+    mod_all,
+    local_sem,
+    x_send,
+    x_recv,
+    f_send,
+    f_recv,
+    g_send,
+    g_recv,
+    o_send,
+    o_recv,
+    e_send,
+    e_recv,
+    m_send,
+    m_recv,
+    wave_send,
+    wave_recv,
+):
+    items, span, width = block_in.shape
+    own = items * span
+    head_pairs = width // 128
+    blocks = active.shape[0]
+    inv_root = HEAD_DIM**-0.5
+    batch, wide = lax.axis_index("batch"), lax.axis_index("wide")
+    z, core = wide // 2, wide % 2
+    y, x = batch // 2, batch % 2
+    zb = z % 2
+
+    def at(y_, x_, z_, core_):
+        return (y_ * 2 + x_, z_ * 2 + core_)
+
+    core_peer = at(y, x, z, 1 - core)
+    x_peer = at(y, 1 - x, z, core)
+    y_peer = at(1 - y, x, z, core)
+    xy_peer = at(1 - y, 1 - x, z, core)
+    z_pair = z + 1 - 2 * zb
+    z1_peer = at(y, x, z_pair, core)
+    z2_peer = at(y, x, (z + 2) % items, core)
+
+    def remote(src, dst, send, recv, device):
+        return pltpu.make_async_remote_copy(
+            src_ref=src,
+            dst_ref=dst,
+            send_sem=send,
+            recv_sem=recv,
+            device_id=device,
+            device_id_type=MESH,
+        )
+
+    def local(src, dst, index):
+        copy = pltpu.make_async_copy(src, dst, local_sem.at[index])
+        copy.start()
+        return copy
+
+    loads = [
+        local(w_ada_in, w_ada, 0),
+        local(w_qkv_in, w_qkv, 1),
+        local(w_proj_in, w_proj, 2),
+        local(w_fc1_in, w_fc1, 3),
+        local(w_fc2_in, w_fc2, 4),
+        local(block_in.at[z], xall.at[0, z], 5),
+        local(cotangent.at[z], gall.at[z], 6),
+    ]
+
+    barrier = pltpu.get_barrier_semaphore()
+    greet = [core_peer, x_peer, y_peer, xy_peer]
+    greet += [at(y, x, (z + step) % items, core) for step in range(1, items)]
+    for device in greet:
+        pl.semaphore_signal(barrier, inc=1, device_id=device, device_id_type=MESH)
+    pl.semaphore_wait(barrier, len(greet))
+
+    x_copies, g_copies = [], []
+    for step in range(1, items):
+        there = (z + step) % items
+        copy = remote(
+            block_in.at[there],
+            xall.at[0, z],
+            x_send.at[step - 1],
+            x_recv.at[step - 1],
+            at(y, x, there, core),
+        )
+        copy.start()
+        x_copies.append(copy)
+    forwards = [
+        remote(block_in.at[z], xall.at[1, z], f_send.at[0], f_recv.at[0], core_peer)
+    ]
+    forwards[0].start()
+    for step in range(1, items):
+        there = (z + step) % items
+        copy = remote(
+            cotangent.at[there],
+            gall.at[z],
+            g_send.at[step - 1],
+            g_recv.at[step - 1],
+            at(y, x, there, core),
+        )
+        copy.start()
+        g_copies.append(copy)
+
+    embed = lead_embed[...].astype(F32)
+    condition = (embed / (1.0 + jnp.exp(-embed))).astype(B16)
+    loads[0].wait()
+    all_rows = dot(condition, w_ada[...], MM) + b_ada[...].astype(F32)
+    mine = lax.broadcasted_iota(jnp.int32, (items, 1), 0) == z
+    mod_rows[...] = jnp.sum(jnp.where(mine, all_rows, 0.0), axis=0, keepdims=True)
+    pieces = [mod_rows[:, column * width : (column + 1) * width] for column in range(6)]
+    shift_att, scale_att, gate_att, shift_mlp, scale_mlp, gate_mlp = pieces
+    mod_own[...] = jnp.zeros(mod_own.shape, F32)
+    mod_own[6:7, :] = jnp.sum(jnp.where(mine, condition.astype(F32), 0.0), axis=0, keepdims=True)
+
+    row = lax.broadcasted_iota(jnp.int32, bias_keys.shape, 0)
+    block_core = jnp.where(row // own == 0, core, 1 - core)
+    position = ((row % own) // span * 2 + block_core) * span + row % span
+    bias_keys[...] = jnp.where(position < lengths[z], 0.0, -1e30)
+
+    loads[5].wait()
+    for step in range(1, items):
+        came = (z + items - step) % items
+        x_copies[step - 1].wait_recv()
+        copy = remote(
+            xall.at[0, came],
+            xall.at[1, came],
+            f_send.at[step],
+            f_recv.at[step],
+            core_peer,
+        )
+        copy.start()
+        forwards.append(copy)
+
+    loads[1].wait()
+    inputs = xall[0].reshape(own, width).astype(F32)
+    normed, norm_inverse = norm_rows(inputs)
+    normed_own[...] = normed
+    entry[:own, :] = (normed * (1.0 + scale_att) + shift_att).astype(B16)
+    q_all[...] = (dot(entry[:own, :], w_qkv[:, :width], MM).astype(B16) * inv_root).astype(B16)
+    kv_all[:own, :] = dot(entry[:own, :], w_qkv[:, width:], MM).astype(B16)
+    for copy in forwards:
+        copy.wait_recv()
+    other_normed, _ = norm_rows(xall[1].reshape(own, width).astype(F32))
+    entry[own:, :] = (other_normed * (1.0 + scale_att) + shift_att).astype(B16)
+    kv_all[own:, :] = dot(entry[own:, :], w_qkv[:, width:], MM).astype(B16)
+
+    lane = lax.broadcasted_iota(jnp.int32, (1, 128), 1)
+    halves = [
+        jnp.where(lane < HEAD_DIM, 1.0, 0.0).astype(B16),
+        jnp.where(lane < HEAD_DIM, 0.0, 1.0).astype(B16),
+    ]
+    for pair in range(head_pairs):
+        lanes = slice(pair * 128, (pair + 1) * 128)
+        v_lanes = slice(width + pair * 128, width + (pair + 1) * 128)
+        keys, values, queries = kv_all[:, lanes], kv_all[:, v_lanes], q_all[:, lanes]
+        parts = []
+        for half in range(2):
+            scores = dot(keys, queries * halves[half], NT) + bias_keys[...]
+            exp_scores = jnp.exp(scores - jnp.max(scores, axis=0, keepdims=True))
+            weights = exp_scores * (1.0 / jnp.sum(exp_scores, axis=0, keepdims=True))
+            probs[pair * 2 + half] = weights
+            out = dot(values, weights.astype(B16), TN)
+            parts.append(out[half * HEAD_DIM : (half + 1) * HEAD_DIM])
+        mixed[:, lanes] = jnp.concatenate(parts, axis=0).T.astype(B16)
+
+    loads[2].wait()
+    branch = dot(mixed[...], w_proj[...], MM)
+    middle = inputs + gate_att * branch
+    middle_ref[0] = branch
+    second_normed, second_inverse = norm_rows(middle)
+    middle_ref[1] = second_normed
+    second = (second_normed * (1.0 + scale_mlp) + shift_mlp).astype(B16)
+    grads_bf[0] = second
+    loads[3].wait()
+    loads[4].wait()
+    mlp_out = jnp.zeros((own, width), F32)
+    for block in range(blocks):
+        columns = slice(block * width, (block + 1) * width)
+        hidden = dot(second, w_fc1[:, columns], MM)
+        cumulative = 0.5 * (1.0 + lax.erf(hidden * (0.5**0.5)))
+        act = (hidden * cumulative).astype(B16)
+        active[block] = act
+        gelu_slope[block] = cumulative + hidden * (
+            jnp.exp(-0.5 * hidden * hidden) * (1.0 / math.sqrt(2.0 * math.pi))
+        )
+        mlp_out = mlp_out + dot(act, w_fc2[columns, :], MM)
+
+    def give_back(values, out, first):
+        send_out[first // items] = values.astype(B16).reshape(items, span, width)
+        copies = []
+        for step in range(1, items):
+            there = (z + step) % items
+            copy = remote(
+                send_out.at[first // items, there],
+                out.at[z],
+                o_send.at[first + step - 1],
+                o_recv.at[first + step - 1],
+                at(y, x, there, core),
+            )
+            copy.start()
+            copies.append(copy)
+        copies.append(local(send_out.at[first // items, z], out.at[z], 7 + first // items))
+        return copies
+
+    block_copies = give_back(middle + gate_mlp * mlp_out, out_block, 0)
+
+    loads[6].wait()
+    for copy in g_copies:
+        copy.wait_recv()
+    gradient = gall[...].reshape(own, width).astype(F32)
+    mod_own[5:6, :] = col_sum(gradient * mlp_out)
+    mlp_grad = (gate_mlp * gradient).astype(B16)
+    grads_bf[1] = mlp_grad
+
+    def wave_copy(wave, slot, src, dst, device):
+        copy = remote(src, dst, wave_send.at[wave, slot], wave_recv.at[wave, slot], device)
+        copy.start()
+        return copy
+
+    def core_start(wave):
+        return wave_copy(wave, 0, core_out.at[wave], core_in.at[wave], core_peer)
+
+    pending = []
+
+    def rows_of(start, count):
+        return pl.ds(pl.multiple_of(start, 16), count)
+
+    def wave_part(wave, part):
+        bits = (x, y) if part == 0 else (y, x)
+        devices = (x_peer, y_peer) if part == 0 else (y_peer, x_peer)
+        slot = 1 + part * 8
+        chunk = hold.shape[1] // 2
+        base = part * chunk
+
+        n1 = chunk // 2
+        away = base + (1 - bits[0]) * n1
+        kept = base + bits[0] * n1
+        stage1[wave, part] = hold[wave, rows_of(away, n1), :].astype(B16)
+        copy1 = wave_copy(wave, slot, stage1.at[wave, part], stage1_in.at[wave, part], devices[0])
+        pending.append(copy1)
+        yield
+        copy1.wait_recv()
+        n2 = n1 // 2
+        away, kept2 = (1 - bits[1]) * n2, bits[1] * n2
+        stage2[wave, part] = (
+            hold[wave, rows_of(kept + away, n2), :]
+            + stage1_in[wave, part, rows_of(away, n2), :].astype(F32)
+        ).astype(B16)
+        copy2 = wave_copy(
+            wave, slot + 1, stage2.at[wave, part], stage2_in.at[wave, part], devices[1]
+        )
+        pending.append(copy2)
+        hold[wave, rows_of(kept + kept2, n2), :] += stage1_in[
+            wave, part, rows_of(kept2, n2), :
+        ].astype(F32)
+        kept = kept + kept2
+        yield
+        copy2.wait_recv()
+        n3 = n2 // 2
+        away, kept3 = (1 - zb) * n3, zb * n3
+        stage3[wave, part] = (
+            hold[wave, rows_of(kept + away, n3), :]
+            + stage2_in[wave, part, rows_of(away, n3), :].astype(F32)
+        ).astype(B16)
+        copy3 = wave_copy(wave, slot + 2, stage3.at[wave, part], stage3_in.at[wave, part], z1_peer)
+        pending.append(copy3)
+        hold[wave, rows_of(kept + kept3, n3), :] += stage2_in[
+            wave, part, rows_of(kept3, n3), :
+        ].astype(F32)
+        place2 = kept
+        kept = kept + kept3
+        yield
+        copy3.wait_recv()
+        stage4[wave, part] = (
+            hold[wave, rows_of(kept, n3), :] + stage3_in[wave, part].astype(F32)
+        ).astype(B16)
+        copy4 = wave_copy(wave, slot + 3, stage4.at[wave, part], stage4_in.at[wave, part], z2_peer)
+        pending.append(copy4)
+        yield
+        copy4.wait_recv()
+        here = core * hold.shape[1]
+        result = total.at[wave, rows_of(here + kept, n3), :]
+        result[...] = (
+            stage4[wave, part].astype(F32) + stage4_in[wave, part].astype(F32)
+        ).astype(B16)
+        copy5 = wave_copy(wave, slot + 4, result, result, z1_peer)
+        pending.append(copy5)
+        yield
+        copy5.wait_recv()
+        result = total.at[wave, rows_of(here + place2, n2), :]
+        copy6 = wave_copy(wave, slot + 5, result, result, devices[1])
+        pending.append(copy6)
+        yield
+        copy6.wait_recv()
+        result = total.at[wave, rows_of(here + base + bits[0] * n1, n1), :]
+        copy7 = wave_copy(wave, slot + 6, result, result, devices[0])
+        pending.append(copy7)
+        yield
+        copy7.wait_recv()
+        result = total.at[wave, rows_of(here + base, chunk), :]
+        copy8 = wave_copy(wave, slot + 7, result, result, core_peer)
+        pending.append(copy8)
+        pending_local.append(put(wave, 2 * core + part, 9 + wave * 4 + part))
+        yield
+        copy8.wait_recv()
+        pending_local.append(put(wave, 2 * (1 - core) + part, 11 + wave * 4 + part))
+
+    pending_local = []
+
+    def put(wave, block, index):
+        rows = rows_of(block * width, width)
+        source = total.at[wave, rows, :]
+        if wave == 0:
+            return local(source, out_fc2.at[rows, :], index)
+        columns = pl.ds(pl.multiple_of(block * width, 128), width)
+        out = out_fc1 if wave == 1 else out_qkvp
+        return local(source, out.at[:, columns], index)
+
+    def core_add(wave, copy):
+        copy.wait_recv()
+        hold[wave] = hold[wave] + core_in[wave].astype(F32)
+
+    def start_parts(wave):
+        parts = [wave_part(wave, 0), wave_part(wave, 1)]
+        for part in parts:
+            next(part)
+        return parts
+
+    def advance(parts):
+        for part in parts:
+            next(part, None)
+
+    per_core = blocks // 2
+    for index in range(per_core):
+        block = (1 - core) * per_core + index
+        rows = slice(index * width, (index + 1) * width)
+        core_out[0, rows, :] = dot(active[block], mlp_grad, TN).astype(B16)
+    copies_core = [core_start(0)]
+    for index in range(per_core):
+        block = core * per_core + index
+        rows = slice(index * width, (index + 1) * width)
+        hold[0, rows, :] = dot(active[block], mlp_grad, TN)
+
+    second_grad = jnp.zeros((own, width), F32)
+    for block in range(blocks):
+        columns = slice(block * width, (block + 1) * width)
+        active_grad = dot(mlp_grad, w_fc2[columns, :], NT)
+        hid = (active_grad * gelu_slope[block]).astype(B16)
+        hidden_grad[block] = hid
+        second_grad = second_grad + dot(hid, w_fc1[:, columns], NT)
+
+    core_add(0, copies_core[0])
+    parts0 = start_parts(0)
+
+    for index in range(per_core):
+        block = (1 - core) * per_core + index
+        rows = slice(index * width, (index + 1) * width)
+        core_out[1, rows, :] = dot(grads_bf[0], hidden_grad[block], TN).astype(B16)
+    copies_core.append(core_start(1))
+    for index in range(per_core):
+        block = core * per_core + index
+        rows = slice(index * width, (index + 1) * width)
+        hold[1, rows, :] = dot(grads_bf[0], hidden_grad[block], TN)
+
+    second_normed = middle_ref[1]
+    mod_own[4:5, :] = col_sum(second_grad * second_normed)
+    mod_own[3:4, :] = col_sum(second_grad)
+    middle_grad = gradient + norm_back(
+        second_normed, second_inverse, second_grad * (1.0 + scale_mlp)
+    )
+    mod_own[2:3, :] = col_sum(middle_grad * middle_ref[0])
+    branch_grad = (gate_att * middle_grad).astype(B16)
+    middle_ref[0] = middle_grad
+    grads_bf[2] = dot(branch_grad, w_proj[...], NT).astype(B16)
+    qkvp[3] = dot(mixed[...], branch_grad, TN)
+
+    core_add(1, copies_core[1])
+    parts1 = start_parts(1)
+
+    dq, dkv = q_all, kv_all
+    for pair in range(head_pairs):
+        lanes = slice(pair * 128, (pair + 1) * 128)
+        v_lanes = slice(width + pair * 128, width + (pair + 1) * 128)
+        keys, values, queries = kv_all[:, lanes], kv_all[:, v_lanes], q_all[:, lanes]
+        out_grad = grads_bf[2, :, lanes]
+        parts = []
+        key_grad = jnp.zeros((2 * own, 128), F32)
+        value_grad = jnp.zeros((2 * own, 128), F32)
+        for half in range(2):
+            masked_grad = out_grad * halves[half]
+            weights = probs[pair * 2 + half]
+            weight_grad = dot(values, masked_grad, NT)
+            score_grad = (
+                weights * (weight_grad - col_sum(weights * weight_grad))
+            ).astype(B16)
+            value_grad = value_grad + dot(weights.astype(B16), masked_grad, MM)
+            key_grad = key_grad + dot(score_grad, queries * halves[half], MM)
+            query_grad = dot(keys, score_grad, TN)
+            parts.append(query_grad[half * HEAD_DIM : (half + 1) * HEAD_DIM])
+        query_grad = jnp.concatenate(parts, axis=0).T * inv_root
+        dq[:, lanes] = query_grad.astype(B16)
+        dkv[:, lanes] = key_grad.astype(B16)
+        dkv[:, v_lanes] = value_grad.astype(B16)
+        if pair == 0:
+            advance(parts0)
+        elif pair == 1:
+            advance(parts1)
+
+    qkvp[0] = dot(entry[:own, :], dq[...], TN)
+    qkvp[1] = dot(entry[...], dkv[:, :width], TN)
+    qkvp[2] = dot(entry[...], dkv[:, width:], TN)
+    for index in range(per_core):
+        rows = slice(index * width, (index + 1) * width)
+        core_out[2, rows, :] = qkvp[(1 - core) * per_core + index].astype(B16)
+        hold[2, rows, :] = qkvp[core * per_core + index]
+    copies_core.append(core_start(2))
+
+    entry_send[...] = dot(dkv[own:, :], w_qkv[:, width:], NT)
+    entry_copy = remote(entry_send, entry_recv, e_send.at[0], e_recv.at[0], core_peer)
+    entry_copy.start()
+    entry_grad = dot(dkv[:own, :], w_qkv[:, width:], NT) + dot(dq[...], w_qkv[:, :width], NT)
+
+    core_add(2, copies_core[2])
+    parts2 = start_parts(2)
+    advance(parts0)
+
+    entry_copy.wait_recv()
+    entry_grad = entry_grad + entry_recv[...]
+    normed = normed_own[...]
+    mod_own[1:2, :] = col_sum(entry_grad * normed)
+    mod_own[0:1, :] = col_sum(entry_grad)
+    mod_copies = [remote(mod_own, mod_in, m_send.at[0], m_recv.at[0], core_peer)]
+    mod_copies[0].start()
+    input_grad = middle_ref[0] + norm_back(normed, norm_inverse, entry_grad * (1.0 + scale_att))
+    input_copies = give_back(input_grad, out_input, items)
+
+    mod_copies[0].wait_recv()
+    first_row = batch * items
+    weight = jnp.where(lax.broadcasted_iota(jnp.int32, mod_own.shape, 0) == 6, 0.5, 1.0)
+    mod_all[first_row + z] = (mod_own[...] + mod_in[...]) * weight
+    for step in range(1, items):
+        there = (z + step) % items
+        place = mod_all.at[first_row + z]
+        copy = remote(place, place, m_send.at[step], m_recv.at[step], at(y, x, there, core))
+        copy.start()
+        mod_copies.append(copy)
+    advance(parts1)
+    advance(parts2)
+    advance(parts0)
+    for copy in mod_copies[1:]:
+        copy.wait_recv()
+    for index, device in enumerate((x_peer, y_peer, xy_peer)):
+        place = mod_all.at[pl.ds(first_row, items)]
+        copy = remote(place, place, m_send.at[items + index], m_recv.at[items + index], device)
+        copy.start()
+        mod_copies.append(copy)
+    advance(parts1)
+    advance(parts2)
+    advance(parts0)
+    for copy in mod_copies[items:]:
+        copy.wait_recv()
+    out_mod[...] = mod_all[...]
+    for _ in range(10):
+        advance(parts1)
+        advance(parts2)
+        advance(parts0)
+
+    for copy in x_copies + g_copies + forwards + copies_core + [entry_copy] + mod_copies + pending:
+        copy.wait_send()
+    for copies in (block_copies, input_copies):
+        for copy in copies[:-1]:
+            copy.wait()
+        copies[-1].wait()
+    for copy in pending_local:
+        copy.wait()
+
+
+def fused(block_in, lead_embed, lengths, w_ada, b_ada, w_qkv, w_proj, w_fc1, w_fc2, cotangent):
+    items, span, width = block_in.shape
+    hidden = w_fc1.shape[1]
+    groups = lax.axis_size("batch")
+    own = items * span
+    blocks = hidden // width
+    half = hidden // 2
+    waves = 3
+    vmem = pl.BlockSpec(memory_space=pltpu.VMEM)
+    smem = pl.BlockSpec(memory_space=pltpu.SMEM)
+    hbm = pl.BlockSpec(memory_space=pl.ANY)
+    chunk = half // 2
+    dma = pltpu.SemaphoreType.DMA
+    scratch = [
+        pltpu.VMEM(w_ada.shape, B16),
+        pltpu.VMEM(w_qkv.shape, B16),
+        pltpu.VMEM(w_proj.shape, B16),
+        pltpu.VMEM(w_fc1.shape, B16),
+        pltpu.VMEM(w_fc2.shape, B16),
+        pltpu.VMEM((2, items, span, width), B16),
+        pltpu.VMEM((items, span, width), B16),
+        pltpu.VMEM((1, 6 * width), F32),
+        pltpu.VMEM((2 * own, width), B16),
+        pltpu.VMEM((own, width), F32),
+        pltpu.VMEM((own, width), B16),
+        pltpu.VMEM((2 * own, 2 * width), B16),
+        pltpu.VMEM((2 * own, own), F32),
+        pltpu.VMEM((HEADS, 2 * own, own), F32),
+        pltpu.VMEM((own, width), B16),
+        pltpu.VMEM((2, own, width), F32),
+        pltpu.VMEM((blocks, own, width), B16),
+        pltpu.VMEM((blocks, own, width), F32),
+        pltpu.VMEM((blocks, own, width), B16),
+        pltpu.VMEM((3, own, width), B16),
+        pltpu.VMEM((2, items, span, width), B16),
+        pltpu.VMEM((own, width), F32),
+        pltpu.VMEM((own, width), F32),
+        pltpu.VMEM((blocks, width, width), F32),
+        pltpu.VMEM((waves, half, width), B16),
+        pltpu.VMEM((waves, half, width), B16),
+        pltpu.VMEM((waves, half, width), F32),
+    ]
+    for divide in (2, 4, 8, 8):
+        scratch += [pltpu.VMEM((waves, 2, chunk // divide, width), B16)] * 2
+    scratch += [
+        pltpu.VMEM((waves, hidden, width), B16),
+        pltpu.VMEM((8, width), F32),
+        pltpu.VMEM((8, width), F32),
+        pltpu.VMEM((groups * items, 8, width), F32),
+        dma((9 + 4 * waves,)),
+        dma((items - 1,)),
+        dma((items - 1,)),
+        dma((items,)),
+        dma((items,)),
+        dma((items - 1,)),
+        dma((items - 1,)),
+        dma((2 * items,)),
+        dma((2 * items,)),
+        dma((1,)),
+        dma((1,)),
+        dma((items + 3,)),
+        dma((items + 3,)),
+        dma((waves, 17)),
+        dma((waves, 17)),
+    ]
+    out_block, out_input, fc2_sum, fc1_sum, qkvp_sum, mod = pl.pallas_call(
+        fused_kernel,
+        out_shape=(
+            jax.ShapeDtypeStruct(block_in.shape, B16),
+            jax.ShapeDtypeStruct(block_in.shape, B16),
+            jax.ShapeDtypeStruct((hidden, width), B16),
+            jax.ShapeDtypeStruct((width, hidden), B16),
+            jax.ShapeDtypeStruct((width, 4 * width), B16),
+            jax.ShapeDtypeStruct((groups * items, 8, width), F32),
+        ),
+        in_specs=[smem, hbm, hbm, vmem, vmem, hbm, hbm, hbm, hbm, hbm],
+        out_specs=(hbm, hbm, hbm, hbm, hbm, vmem),
+        scratch_shapes=scratch,
+        name="fused_block",
+        compiler_params=pltpu.CompilerParams(
+            collective_id=0, has_side_effects=True, vmem_limit_bytes=56 * 2**20
+        ),
+    )(
+        lengths,
+        block_in,
+        cotangent,
+        lead_embed,
+        b_ada.reshape(1, -1),
+        w_ada,
+        w_qkv,
+        w_proj,
+        w_fc1,
+        w_fc2,
+    )
+    pieces = mod[:, :6].reshape(groups * items, 6 * width)
+    ada_grad = lax.dot_general(mod[:, 6], pieces, TN, precision=lax.Precision.HIGHEST)
+    return (
+        out_block.astype(F32),
+        out_input.astype(F32),
+        ada_grad,
+        jnp.sum(pieces, axis=0),
+        qkvp_sum[:, : 3 * width].astype(F32),
+        qkvp_sum[:, 3 * width :].astype(F32),
+        fc1_sum.astype(F32),
+        fc2_sum.astype(F32),
+    )
+
+
+def choose(*arrays):
+    items, span, width = arrays[0].shape
+    fits = (
+        lax.axis_size("batch") == 4
+        and items == 4
+        and lax.axis_size("wide") == 2 * items
+        and span == 64
+        and width == HEADS * HEAD_DIM == 384
+        and arrays[7].shape[1] == 4 * width
+    )
+    return (fused if fits else on_device)(*arrays)
+
+
 def solution(mesh):
     return jax.shard_map(
-        on_device,
+        choose,
         mesh=mesh,
         in_specs=(
             P("batch", "wide", None),

time: 538 us -> 94.4 us (0.18); the launches traced: 529 us -> 93.4 us
  waiting for transfers between devices: 230 us -> 0 us
  local copies, waits for them, and re-layouts: 181 us -> 2.99 us
  Pallas kernels: 0 us -> 75.3 us
  blocking collectives: 39.2 us -> 0 us
  matrix products: 28.7 us -> 4.75 us
  starting transfers between devices: 21.8 us -> 0 us
  between operations: 15.4 us -> 0.66 us
    psum x1 -> x0, waiting for transfers between devices: 178 us -> none  [on_device(): lax.psum((ada_grad, bias_grad, qkv_grad, proj_grad, fc1_grad, fc2_grad),...]
    unnamed x116 -> x7, local copies, waits for them, and re-layouts: 77.8 us -> 0.04 us
    pallas_call x0 -> x1, Pallas kernels: none -> 75.3 us  [fused(): pl.pallas_call(fused_kernel, out_shape=(jax.ShapeDtypeStruct(block_in.sha...]
    all_to_all x5 -> x0, waiting for transfers between devices: 52.2 us -> none  [the longest x1 16.9 us: on_device(): lax.all_to_all(to_heads(triple, 3, head_count, head_size), 'wide', split_...]
    all_to_all x7 -> x0, local copies, waits for them, and re-layouts: 48.6 us -> none  [the longest x1 42.2 us: on_device(): lax.all_to_all(triple_grad.reshape(3, pair_count, slot_len * head_size),...]
    psum x1 -> x0, blocking collectives: 39.2 us -> none  [on_device(): lax.psum((ada_grad, bias_grad, qkv_grad, proj_grad, fc1_grad, fc2_grad),...]
    another operation x8 -> x0, local copies, waits for them, and re-layouts: 35.2 us -> none  [the longest x4 34.2 us: attend_backward(): jnp.stack([join_rows(query_grads), key_grad, value_grad])]
    dot_general x22 -> x1, matrix products: 28.7 us -> 4.75 us  [fused(): lax.dot_general(mod[:, 6], pieces, TN, precision=lax.Precision.HIGHEST)]
  transfers between devices with their start and end apart: 6 -> 0, of which waited for: 6 -> 0; matrix products, arithmetic and copies ran while one was open for 5% -> 0% of each run, Pallas kernels for 0% -> 0%
where the time goes in v1:
time: 94.4 us; the launch traced here: 93.4 us
  Pallas kernels  75.3 us (80%)
  other arithmetic  9.78 us (10%)
  matrix products  4.75 us (5%)
  local copies, waits for them, and re-layouts  2.99 us (3%)
    pallas_call x1, Pallas kernels, fused(): pl.pallas_call(fused_kernel, out_shape=(jax.ShapeDtypeStruct(block_in.sha...  75.3 us
    dot_general x1, matrix products, fused(): lax.dot_general(mod[:, 6], pieces, TN, precision=lax.Precision.HIGHEST)  4.75 us

profile of v1, /device:TPU:0, one launch (start us, length us, event | category | flops | bytes accessed | tf_op | source)
XLA Modules:
  0.0 93.4 jit_solution(402085367027948375)
XLA Ops:
  0.6 1.3 %reshape.23.b_ada = bf16[1,2304]{1,0:T(2,128)(2,1)} reshape(bf16[2304]{0:T(1024)(128)(2,1)} %param.14) | data formatting | bytes 9216 | tf_op jit(solution)/shard_map/reshape | solution.py:890
  1.9 75.3 %fused_block.1 = (bf16[4,64,384]{2,1,0:T(8,128)(2,1)}, bf16[4,64,384]{2,1,0:T(8,128)(2,1)}, bf16[1536,384]{1,0:T(8,128)(2,1)}, bf16[384,1536]{1,0:T(8,128)(2,1)}...) custom-call(s32[4]{0:T(128)} %lengths.1, bf16[4,64,384]{2,1,0:T(8,128)(2,1)} %block_in.1, ...), custom_call_target="tpu_custom_call" | custom-call | tf_op jit(solution)/shard_map/fused_block/pallas_call | solution.py:868
  77.2 0.0 copy-start.2
  77.2 1.0 %slice.12 = f32[16,1,384]{2,1,0:T(1,128)S(1)} slice(f32[16,8,384]{2,1,0:T(8,128)} %get-tuple-element.16), slice={[0:16], [6:7], [0:384]} | slice | bytes 49152 | tf_op jit(solution)/shard_map/slice | solution.py:898
  78.2 1.0 %slice_reduce_fusion = (f32[6,384]{1,0:T(8,128)S(1)}, f32[16,6,384]{2,1,0:T(8,128)S(1)}) fusion(f32[16,8,384]{2,1,0:T(8,128)} %get-tuple-element.16), kind=kLoop, calls=%fused_computation.5 | loop fusion | flops 34560 | bytes 304128 | tf_op jit(solution)/shard_map/reduce_sum | solution.py:903
  79.2 0.6 reduce_sum.12
  79.8 1.7 %convert_element_type.18 = f32[4,64,384]{2,1,0:T(8,128)} convert(bf16[4,64,384]{2,1,0:T(8,128)(2,1)} %get-tuple-element.14) | non-fusion elementwise | flops 98304 | bytes 589824 | tf_op jit(solution)/shard_map/convert_element_type | solution.py:900
  81.5 1.7 %convert_element_type.19 = f32[4,64,384]{2,1,0:T(8,128)} convert(bf16[4,64,384]{2,1,0:T(8,128)(2,1)} %get-tuple-element.15) | non-fusion elementwise | flops 98304 | bytes 589824 | tf_op jit(solution)/shard_map/convert_element_type | solution.py:901
  83.2 0.0 copy-done.2
  83.2 0.0 copy-start.1
  83.2 0.9 slice_convert_fusion.1
  84.1 1.3 %slice_convert_fusion = f32[384,1152]{1,0:T(8,128)} fusion(bf16[384,1536]{1,0:T(8,128)(2,1)S(1)} %copy-done.2), kind=kLoop, calls=%fused_computation | loop fusion | flops 442368 | bytes 2654208 | tf_op jit(solution)/shard_map/convert_element_type | solution.py:904
  85.4 0.0 copy-done.1
  85.4 0.0 copy-start
  85.4 1.7 %convert_element_type.22 = f32[384,1536]{1,0:T(8,128)} convert(bf16[384,1536]{1,0:T(8,128)(2,1)S(1)} %copy-done.1) | non-fusion elementwise | flops 589824 | bytes 3538944 | tf_op jit(solution)/shard_map/convert_element_type | solution.py:906
  87.1 0.0 copy-done
  87.1 1.6 %convert_element_type.23 = f32[1536,384]{1,0:T(8,128)} convert(bf16[1536,384]{1,0:T(8,128)(2,1)S(1)} %copy-done) | non-fusion elementwise | flops 589824 | bytes 3538944 | tf_op jit(solution)/shard_map/convert_element_type | solution.py:907
  88.7 4.8 %fusion = f32[384,2304]{1,0:T(8,128)} fusion(f32[16,2304]{1,0:T(8,128)S(1)} %bitcast.7, f32[16,1,384]{2,1,0:T(1,128)S(1)} %slice.12), kind=kOutput, calls=%fused_computation.2 | convolution fusion | flops 169869312 | bytes 3710976 | tf_op jit(solution)/shard_map/dot_general | solution.py:898
  (1 shorter events, 0.0 us)
Async XLA Ops:
  77.2 6.1 %copy-start.2 = (bf16[384,1536]{1,0:T(8,128)(2,1)S(1)}, bf16[384,1536]{1,0:T(8,128)(2,1)}, u32[]{:S(2)}) copy-start(bf16[384,1536]{1,0:T(8,128)(2,1)} %get-tuple-element.17) | copy-start | bytes 3538948
  83.2 2.2 %copy-start.1 = (bf16[384,1536]{1,0:T(8,128)(2,1)S(1)}, bf16[384,1536]{1,0:T(8,128)(2,1)}, u32[]{:S(2)}) copy-start(bf16[384,1536]{1,0:T(8,128)(2,1)} %get-tuple-element.18) | copy-start | bytes 3538948
  85.4 1.7 %copy-start = (bf16[1536,384]{1,0:T(8,128)(2,1)S(1)}, bf16[1536,384]{1,0:T(8,128)(2,1)}, u32[]{:S(2)}) copy-start(bf16[1536,384]{1,0:T(8,128)(2,1)} %get-tuple-element.19) | copy-start | bytes 3538948

commit v2 on v0

--- a/solution.py
+++ b/solution.py
@@ -1,8 +1,11 @@
+import math
 from functools import partial
 
 import jax
 import jax.numpy as jnp
 from jax import lax
+from jax.experimental import pallas as pl
+from jax.experimental.pallas import tpu as pltpu
 from jax.sharding import PartitionSpec as P
 
 HEADS = 6
@@ -254,9 +257,909 @@
     return (block_out, input_grad, totals[0], totals[1], totals[2], totals[3], totals[4], totals[5])
 
 
+MESH = pl.DeviceIdType.MESH
+MM = (((1,), (0,)), ((), ()))
+NT = (((1,), (1,)), ((), ()))
+TN = (((0,), (0,)), ((), ()))
+B16 = jnp.bfloat16
+F32 = jnp.float32
+
+STREAMS = (
+    (0, 0, 256, "zpqZ"),
+    (0, 256, 128, "pqzZ"),
+    (0, 384, 256, "pqzZ"),
+    (0, 640, 128, "pzZq"),
+    (1, 0, 256, "D"),
+    (1, 256, 256, "pqzZ"),
+    (1, 512, 256, "zpqZ"),
+    (2, 0, 256, "pqzZ"),
+    (2, 256, 128, "pzqZ"),
+    (2, 384, 256, "pqzZ"),
+    (2, 640, 128, "zpqZ"),
+)
+ORDER = (
+    -1, -1, -1, -1, -1, -1, -1, -1, 0, 1, 2, 3, -1, -1, -1, 4, 5, 6, -1, 1,
+    7, 8, 3, 0, 2, -1, -1, 4, 6, 3, 9, 10, 1, -1, 8, 0, 2, -1, 5, 4,
+    1, 7, 6, 3, 9, 10, 0, 8, -1, 2, 5, 3, 6, 4, 7, 1, 8, 10, 9, 0,
+    5, -1, 2, 3, 1, 10, 7, 6, 8, 4, 9, 0, 2, 5, 3, 4, 1, 6, 8, 10,
+    0, 7, 2, 5, 9, 3, 8, 10, 1, 6, 3, 1, 7, 5, 9, 10, 2, 8, -1, 0,
+    2, 8, 7, 0, 6, 9, 5, 6, 5, 7, 10, 9, 7, 10, 9,
+)
+
+
+def dot(left, right, dims):
+    return lax.dot_general(left, right, dims, preferred_element_type=F32)
+
+
+def col_sum(values):
+    return jnp.sum(values, axis=0, keepdims=True)
+
+
+def fused_kernel(
+    lengths_in,
+    block_in,
+    cotangent,
+    lead_embed_in,
+    b_ada_in,
+    w_ada_in,
+    w_qkv_in,
+    w_proj_in,
+    w_fc1_in,
+    w_fc2_in,
+    out_block,
+    out_input,
+    out_fc2,
+    out_fc1,
+    out_qkvp,
+    out_mod,
+    lengths,
+    lead_embed,
+    b_ada,
+    w_ada,
+    w_qkv,
+    w_proj,
+    w_fc1,
+    w_fc2,
+    xall,
+    gall,
+    mod_rows,
+    entry,
+    normed_own,
+    q_all,
+    kv_all,
+    bias_keys,
+    probs,
+    inverses,
+    mixed,
+    branch_ref,
+    second_ref,
+    active,
+    gelu_slope,
+    hidden_grad,
+    grads_bf,
+    send_out,
+    entry_send,
+    entry_recv,
+    qkvp,
+    core_out,
+    core_in,
+    hold,
+    stage,
+    stage_in,
+    total,
+    mod_own,
+    mod_in,
+    mod_all,
+    load_sem,
+    put_sem,
+    x_send,
+    x_recv,
+    f_send,
+    f_recv,
+    g_send,
+    g_recv,
+    o_send,
+    o_recv,
+    e_send,
+    e_recv,
+    m_send,
+    m_recv,
+    c_send,
+    c_recv,
+    s_send,
+    s_recv,
+):
+    items, span, width = block_in.shape
+    own = items * span
+    head_pairs = width // 128
+    blocks = active.shape[0]
+    half_rows = hold.shape[1]
+    inv_root = HEAD_DIM**-0.5
+    batch, wide = lax.axis_index("batch"), lax.axis_index("wide")
+    z, core = wide // 2, wide % 2
+    y, x = batch // 2, batch % 2
+    zb = z % 2
+
+    def at(y_, x_, z_, core_):
+        return (y_ * 2 + x_, z_ * 2 + core_)
+
+    core_peer = at(y, x, z, 1 - core)
+    x_peer = at(y, 1 - x, z, core)
+    y_peer = at(1 - y, x, z, core)
+    xy_peer = at(1 - y, 1 - x, z, core)
+    flip_x, flip_y = 1 - 2 * x, 1 - 2 * y
+    peers = {
+        "p": at(y + flip_y * core, x + flip_x * (1 - core), z, core),
+        "q": at(y + flip_y * (1 - core), x + flip_x * core, z, core),
+        "z": at(y, x, z + 1 - 2 * zb, core),
+        "Z": at(y, x, (z + 2) % items, core),
+    }
+    sides = {
+        "p": x * (1 - core) + y * core,
+        "q": y * (1 - core) + x * core,
+        "z": zb,
+        "Z": z // 2,
+    }
+
+    def remote(src, dst, send, recv, device):
+        copy = pltpu.make_async_remote_copy(
+            src_ref=src,
+            dst_ref=dst,
+            send_sem=send,
+            recv_sem=recv,
+            device_id=device,
+            device_id_type=MESH,
+        )
+        copy.start()
+        return copy
+
+    def load(src, dst, index):
+        copy = pltpu.make_async_copy(src, dst, load_sem.at[index])
+        copy.start()
+        return copy
+
+    puts = []
+
+    def put(src, dst):
+        copy = pltpu.make_async_copy(src, dst, put_sem.at[len(puts)])
+        copy.start()
+        puts.append(copy)
+
+    barrier = pltpu.get_barrier_semaphore()
+    greet = [core_peer, x_peer, y_peer, xy_peer]
+    greet += [at(y, x, (z + step) % items, core) for step in range(1, items)]
+    for device in greet:
+        pl.semaphore_signal(barrier, inc=1, device_id=device, device_id_type=MESH)
+    loads = [
+        load(block_in.at[z], xall.at[0, z], 0),
+        load(w_ada_in, w_ada, 1),
+        load(w_qkv_in, w_qkv, 2),
+        load(w_proj_in, w_proj, 3),
+        load(w_fc1_in, w_fc1, 4),
+        load(w_fc2_in, w_fc2, 5),
+        load(cotangent.at[z], gall.at[z], 6),
+        load(lead_embed_in, lead_embed, 7),
+        load(b_ada_in, b_ada, 8),
+        load(lengths_in, lengths, 9),
+    ]
+    pl.semaphore_wait(barrier, len(greet))
+
+    x_copies, g_copies = [], []
+    for step in range(1, items):
+        there = (z + step) % items
+        x_copies.append(
+            remote(
+                block_in.at[there],
+                xall.at[0, z],
+                x_send.at[step - 1],
+                x_recv.at[step - 1],
+                at(y, x, there, core),
+            )
+        )
+    forwards = [
+        remote(block_in.at[z], xall.at[1, z], f_send.at[0], f_recv.at[0], core_peer)
+    ]
+
+    for index in (7, 8, 9):
+        loads[index].wait()
+    embed = lead_embed[...].astype(F32)
+    condition = (embed / (1.0 + jnp.exp(-embed))).astype(B16)
+    loads[1].wait()
+    all_rows = dot(condition, w_ada[...], MM) + b_ada[...].astype(F32).reshape(1, -1)
+    mine = lax.broadcasted_iota(jnp.int32, (items, 1), 0) == z
+    mod_rows[...] = jnp.sum(jnp.where(mine, all_rows, 0.0), axis=0, keepdims=True)
+    pieces = [mod_rows[:, column * width : (column + 1) * width] for column in range(6)]
+    shift_att, scale_att, gate_att, shift_mlp, scale_mlp, gate_mlp = pieces
+    mod_own[...] = jnp.zeros(mod_own.shape, F32)
+    inverses[...] = jnp.zeros(inverses.shape, F32)
+    mod_own[6:7, :] = jnp.sum(jnp.where(mine, condition.astype(F32), 0.0), axis=0, keepdims=True)
+
+    lane = lax.broadcasted_iota(jnp.int32, (1, 128), 1)
+    halves, marks = [], []
+    row = lax.broadcasted_iota(jnp.int32, (2 * own, 128), 0)
+    block_core = jnp.where(row // own == 0, core, 1 - core)
+    position = ((row % own) // span * 2 + block_core) * span + row % span
+    bias = jnp.where(position < lengths[z], 0.0, -1e30)
+    for half in range(2):
+        inside = lane // HEAD_DIM == half
+        halves.append(jnp.where(inside, 1.0, 0.0).astype(B16))
+        mark = jnp.where(lane == (1 - half) * HEAD_DIM, 1.0, 0.0)
+        marks.append(mark.astype(B16))
+        bias_keys[half] = (bias * mark).astype(B16)
+
+    loads[0].wait()
+    for step in range(1, items):
+        came = (z + items - step) % items
+        x_copies[step - 1].wait_recv()
+        forwards.append(
+            remote(
+                xall.at[0, came],
+                xall.at[1, came],
+                f_send.at[step],
+                f_recv.at[step],
+                core_peer,
+            )
+        )
+    for step in range(1, items):
+        there = (z + step) % items
+        g_copies.append(
+            remote(
+                cotangent.at[there],
+                gall.at[z],
+                g_send.at[step - 1],
+                g_recv.at[step - 1],
+                at(y, x, there, core),
+            )
+        )
+
+    loads[2].wait()
+    inputs = xall[0].reshape(own, width).astype(F32)
+    normed, norm_inverse = norm_rows(inputs)
+    normed_own[...] = normed
+    entry[:own, :] = (normed * (1.0 + scale_att) + shift_att).astype(B16)
+    q_all[...] = (dot(entry[:own, :], w_qkv[:, :width], MM).astype(B16) * inv_root).astype(B16)
+    kv_all[:own, :] = dot(entry[:own, :], w_qkv[:, width:], MM).astype(B16)
+    for copy in forwards:
+        copy.wait_recv()
+    other_normed, _ = norm_rows(xall[1].reshape(own, width).astype(F32))
+    entry[own:, :] = (other_normed * (1.0 + scale_att) + shift_att).astype(B16)
+    kv_all[own:, :] = dot(entry[own:, :], w_qkv[:, width:], MM).astype(B16)
+
+    for pair in range(head_pairs):
+        lanes = slice(pair * 128, (pair + 1) * 128)
+        v_lanes = slice(width + pair * 128, width + (pair + 1) * 128)
+        keys, values, queries = kv_all[:, lanes], kv_all[:, v_lanes], q_all[:, lanes]
+        parts = []
+        for half in range(2):
+            head = pair * 2 + half
+            scores = dot(
+                keys * halves[half] + bias_keys[half], queries * halves[half] + marks[half], NT
+            )
+            exp_scores = jnp.exp(scores - jnp.max(scores, axis=0, keepdims=True))
+            inverse = 1.0 / jnp.sum(exp_scores, axis=0, keepdims=True)
+            inverses[head : head + 1, :] = inverse
+            weights = exp_scores.astype(B16)
+            probs[head] = weights
+            out = dot(values, weights, TN)[half * HEAD_DIM : (half + 1) * HEAD_DIM] * inverse
+            parts.append(out)
+        mixed[:, lanes] = jnp.concatenate(parts, axis=0).T.astype(B16)
+
+    loads[3].wait()
+    branch = dot(mixed[...], w_proj[...], MM)
+    middle = inputs + gate_att * branch
+    branch_ref[...] = branch
+    second_normed, second_inverse = norm_rows(middle)
+    second_ref[...] = second_normed
+    second = (second_normed * (1.0 + scale_mlp) + shift_mlp).astype(B16)
+    grads_bf[0] = second
+    loads[4].wait()
+    loads[5].wait()
+    mlp_out = jnp.zeros((own, width), F32)
+    for block in range(blocks):
+        columns = slice(block * width, (block + 1) * width)
+        hidden = dot(second, w_fc1[:, columns], MM)
+        cumulative = 0.5 * (1.0 + lax.erf(hidden * (0.5**0.5)))
+        act = (hidden * cumulative).astype(B16)
+        active[block] = act
+        gelu_slope[block] = cumulative + hidden * (
+            jnp.exp(-0.5 * hidden * hidden) * (1.0 / math.sqrt(2.0 * math.pi))
+        )
+        mlp_out = mlp_out + dot(act, w_fc2[columns, :], MM)
+
+    outs = []
+
+    def give_back(out, which):
+        for step in range(1, items):
+            there = (z + step) % items
+            slot = which * items + step
+            outs.append(
+                remote(
+                    send_out.at[which, there],
+                    out.at[z],
+                    o_send.at[slot],
+                    o_recv.at[slot],
+                    at(y, x, there, core),
+                )
+            )
+        put(send_out.at[which, z], out.at[z])
+
+    def rows_of(start, count):
+        return pl.ds(pl.multiple_of(start, 16), count)
+
+    core_copies = {}
+    core_done = set()
+    sent = []
+
+    def core_start(wave, first, count):
+        rows = pl.ds(first, count)
+        core_copies[wave, first] = remote(
+            core_out.at[wave, rows],
+            core_in.at[wave, rows],
+            c_send.at[len(core_copies)],
+            c_recv.at[len(core_copies)],
+            core_peer,
+        )
+
+    def write_out(wave, at_core, base, count):
+        first = at_core * half_rows + base
+        if wave == 0:
+            rows = rows_of(first, count)
+            put(total.at[wave, rows, :], out_fc2.at[rows, :])
+            return
+        done = 0
+        while done < count:
+            block, inside = divmod(base + done, width)
+            size = min(count - done, width - inside)
+            rows, out_rows = rows_of(first + done, size), pl.ds(inside, size)
+            if wave == 1:
+                columns = pl.ds(pl.multiple_of((at_core * 2 + block) * width, 128), width)
+                put(total.at[wave, rows, :], out_fc1.at[out_rows, columns])
+            else:
+                if block == 0:
+                    start, stride = at_core * 3 * width, width - at_core * (width - 128)
+                else:
+                    start, stride = 128 + at_core * 128, width
+                for piece in range(3):
+                    columns = pl.ds(pl.multiple_of(start + piece * stride, 128), 128)
+                    put(
+                        total.at[wave, rows, pl.ds(piece * 128, 128)],
+                        out_qkvp.at[out_rows, columns],
+                    )
+            done += size
+
+    groups = {
+        "xy": (y * 2 + x, ((y * 2 + 1 - x, x_peer), (2 - y * 2 + x, y_peer), (3 - y * 2 - x, xy_peer))),
+        "z": (
+            z,
+            tuple(
+                ((z + step) % items, at(y, x, (z + step) % items, core)) for step in range(1, items)
+            ),
+        ),
+    }
+
+    def direct(index, wave, base, count, order):
+        slot, kept, size, place = 0, base, count, base
+        before = core_in
+        places = []
+        for name in order:
+            side, others = groups[name]
+            size //= 4
+            copies = []
+            for number, (other, device) in reversed(list(enumerate(others))):
+                away = kept + other * size
+                area = pl.ds(place + number * size, size)
+                values = hold[wave, rows_of(away, size), :]
+                if before is not None:
+                    values = values + before[wave, rows_of(away, size), :].astype(F32)
+                stage[wave, area, :] = values.astype(B16)
+                copies.append(
+                    remote(
+                        stage.at[wave, area],
+                        stage_in.at[wave, area],
+                        s_send.at[index, slot],
+                        s_recv.at[index, slot],
+                        device,
+                    )
+                )
+                slot += 1
+            sent.extend(copies)
+            kept = kept + side * size
+            yield
+            for copy in copies:
+                copy.wait_recv()
+            values = hold[wave, rows_of(kept, size), :]
+            if before is not None:
+                values = values + before[wave, rows_of(kept, size), :].astype(F32)
+            for number in range(3):
+                area = pl.ds(place + number * size, size)
+                values = values + stage_in[wave, area, :].astype(F32)
+            if len(places) == 0:
+                hold[wave, rows_of(kept, size), :] = values
+            else:
+                total[wave, rows_of(core * half_rows + kept, size), :] = values.astype(B16)
+            places.append((others, kept, size))
+            before, place = None, place + 3 * size
+        for others, start, size in reversed(places):
+            area = total.at[wave, rows_of(core * half_rows + start, size)]
+            copies = []
+            for _, device in reversed(others):
+                copies.append(
+                    remote(area, area, s_send.at[index, slot], s_recv.at[index, slot], device)
+                )
+                slot += 1
+            sent.extend(copies)
+            yield
+            for copy in copies:
+                copy.wait_recv()
+        area = total.at[wave, rows_of(core * half_rows + base, count)]
+        copy = remote(area, area, s_send.at[index, slot], s_recv.at[index, slot], core_peer)
+        sent.append(copy)
+        write_out(wave, core, base, count)
+        yield
+        copy.wait_recv()
+        write_out(wave, 1 - core, base, count)
+
+    def stream(index, wave, base, count, dims):
+        keys = [first for kept_wave, first in core_copies if kept_wave == wave]
+        for key in [first for first in keys if first < base + count]:
+            if (wave, key) in core_done:
+                continue
+            core_done.add((wave, key))
+            core_copies[wave, key].wait_recv()
+        if dims in "DE":
+            yield from direct(index, wave, base, count, ("xy", "z") if dims == "D" else ("z", "xy"))
+            return
+        slot = 0
+        kept, size, place = base, count, base
+        before, before_at = core_in, base
+        places = []
+        for dim in dims[:-1]:
+            size //= 2
+            away, keep = (1 - sides[dim]) * size, sides[dim] * size
+            area = pl.ds(place, size)
+            stage[wave, area, :] = (
+                hold[wave, rows_of(kept + away, size), :]
+                + before[wave, rows_of(before_at + away, size), :].astype(F32)
+            ).astype(B16)
+            copy = remote(
+                stage.at[wave, area],
+                stage_in.at[wave, area],
+                s_send.at[index, slot],
+                s_recv.at[index, slot],
+                peers[dim],
+            )
+            sent.append(copy)
+            hold[wave, rows_of(kept + keep, size), :] += before[
+                wave, rows_of(before_at + keep, size), :
+            ].astype(F32)
+            places.append((dim, kept + keep, size))
+            kept, slot = kept + keep, slot + 1
+            before, before_at, place = stage_in, place, place + size
+            yield
+            copy.wait_recv()
+        area = pl.ds(place, size)
+        stage[wave, area, :] = (
+            hold[wave, rows_of(kept, size), :]
+            + before[wave, rows_of(before_at, size), :].astype(F32)
+        ).astype(B16)
+        copy = remote(
+            stage.at[wave, area],
+            stage_in.at[wave, area],
+            s_send.at[index, slot],
+            s_recv.at[index, slot],
+            peers[dims[-1]],
+        )
+        sent.append(copy)
+        slot += 1
+        yield
+        copy.wait_recv()
+        here = core * half_rows
+        total[wave, rows_of(here + kept, size), :] = (
+            stage[wave, area, :].astype(F32) + stage_in[wave, area, :].astype(F32)
+        ).astype(B16)
+        for dim, start, size in reversed(places):
+            area = total.at[wave, rows_of(here + start, size)]
+            copy = remote(area, area, s_send.at[index, slot], s_recv.at[index, slot], peers[dim])
+            sent.append(copy)
+            slot += 1
+            yield
+            copy.wait_recv()
+        area = total.at[wave, rows_of(here + base, count)]
+        copy = remote(area, area, s_send.at[index, slot], s_recv.at[index, slot], core_peer)
+        sent.append(copy)
+        write_out(wave, core, base, count)
+        yield
+        copy.wait_recv()
+        write_out(wave, 1 - core, base, count)
+
+    def compute():
+        per_core = blocks // 2
+        block_result = middle + gate_mlp * mlp_out
+        send_out[0] = block_result.astype(B16).reshape(items, span, width)
+        loads[6].wait()
+        for copy in g_copies:
+            copy.wait_recv()
+        gradient = gall[...].reshape(own, width).astype(F32)
+        mlp_grad = (gate_mlp * gradient).astype(B16)
+        grads_bf[1] = mlp_grad
+        for index in range(per_core):
+            block = (1 - core) * per_core + index
+            rows = slice(index * width, (index + 1) * width)
+            core_out[0, rows, :] = dot(active[block], mlp_grad, TN).astype(B16)
+        core_start(0, 0, half_rows)
+        yield
+        for index in range(per_core):
+            block = core * per_core + index
+            rows = slice(index * width, (index + 1) * width)
+            hold[0, rows, :] = dot(active[block], mlp_grad, TN)
+        yield
+        second_grad = jnp.zeros((own, width), F32)
+        for block in range(blocks):
+            columns = slice(block * width, (block + 1) * width)
+            active_grad = dot(mlp_grad, w_fc2[columns, :], NT)
+            hid = (active_grad * gelu_slope[block]).astype(B16)
+            hidden_grad[block] = hid
+            second_grad = second_grad + dot(hid, w_fc1[:, columns], NT)
+            yield
+        for index in range(per_core):
+            block = (1 - core) * per_core + index
+            rows = slice(index * width, (index + 1) * width)
+            core_out[1, rows, :] = dot(grads_bf[0], hidden_grad[block], TN).astype(B16)
+        core_start(1, 0, half_rows)
+        yield
+        for index in range(per_core):
+            block = core * per_core + index
+            rows = slice(index * width, (index + 1) * width)
+            hold[1, rows, :] = dot(grads_bf[0], hidden_grad[block], TN)
+        yield
+        second_normed = second_ref[...]
+        middle_grad = gradient + norm_back(
+            second_normed, second_inverse, second_grad * (1.0 + scale_mlp)
+        )
+        branch_grad = (gate_att * middle_grad).astype(B16)
+        grads_bf[2] = dot(branch_grad, w_proj[...], NT).astype(B16)
+        qkvp[3] = dot(mixed[...], branch_grad, TN)
+        yield
+        mod_own[5:6, :] = col_sum(gradient * mlp_out)
+        mod_own[4:5, :] = col_sum(second_grad * second_normed)
+        mod_own[3:4, :] = col_sum(second_grad)
+        mod_own[2:3, :] = col_sum(middle_grad * branch_ref[...])
+        yield
+
+        dq, dkv = q_all, kv_all
+        inverse_columns = inverses[...].T
+        for pair in range(head_pairs):
+            lanes = slice(pair * 128, (pair + 1) * 128)
+            v_lanes = slice(width + pair * 128, width + (pair + 1) * 128)
+            keys, values, queries = kv_all[:, lanes], kv_all[:, v_lanes], q_all[:, lanes]
+            out_grad = grads_bf[2, :, lanes].astype(F32)
+            parts = []
+            key_grad = jnp.zeros((2 * own, 128), F32)
+            value_grad = jnp.zeros((2 * own, 128), F32)
+            for half in range(2):
+                head = pair * 2 + half
+                masked_grad = (
+                    out_grad * inverse_columns[:, head : head + 1] * halves[half].astype(F32)
+                ).astype(B16)
+                weights = probs[head]
+                wide_weights = weights.astype(F32)
+                weight_grad = dot(values, masked_grad, NT)
+                row_sum = col_sum(wide_weights * weight_grad) * inverses[head : head + 1, :]
+                score_grad = (wide_weights * (weight_grad - row_sum)).astype(B16)
+                value_grad = value_grad + dot(weights, masked_grad, MM)
+                key_grad = key_grad + dot(score_grad, queries * halves[half], MM)
+                query_grad = dot(keys, score_grad, TN)
+                parts.append(query_grad[half * HEAD_DIM : (half + 1) * HEAD_DIM])
+            query_grad = jnp.concatenate(parts, axis=0).T * inv_root
+            dq[:, lanes] = query_grad.astype(B16)
+            dkv[:, lanes] = key_grad.astype(B16)
+            dkv[:, v_lanes] = value_grad.astype(B16)
+            qkvp[pair, :, :128] = dot(entry[:own, :], dq[:, lanes], TN)
+            qkvp[pair, :, 128:256] = dot(entry[...], dkv[:, lanes], TN)
+            qkvp[pair, :, 256:] = dot(entry[...], dkv[:, v_lanes], TN)
+            if pair == 0:
+                core_out[2, :width, :] = qkvp[3 * (1 - core)].astype(B16)
+                core_start(2, 0, width)
+                hold[2, :width, :] = qkvp[3 * core]
+            elif pair == 2:
+                core_out[2, width:, :] = qkvp[2 - core].astype(B16)
+                core_start(2, width, width)
+                hold[2, width:, :] = qkvp[1 + core]
+            yield
+
+        entry_send[...] = dot(dkv[own:, :], w_qkv[:, width:], NT)
+        entry_copy = remote(entry_send, entry_recv, e_send.at[0], e_recv.at[0], core_peer)
+        sent.append(entry_copy)
+        entry_grad = dot(dkv[:own, :], w_qkv[:, width:], NT) + dot(dq[...], w_qkv[:, :width], NT)
+        yield
+        entry_copy.wait_recv()
+        entry_grad = entry_grad + entry_recv[...]
+        normed = normed_own[...]
+        mod_own[1:2, :] = col_sum(entry_grad * normed)
+        mod_own[0:1, :] = col_sum(entry_grad)
+        mod_copy = remote(mod_own, mod_in, m_send.at[0], m_recv.at[0], core_peer)
+        sent.append(mod_copy)
+        input_grad = middle_grad + norm_back(
+            normed, norm_inverse, entry_grad * (1.0 + scale_att)
+        )
+        send_out[1] = input_grad.astype(B16).reshape(items, span, width)
+        yield
+        mod_copy.wait_recv()
+        first_row = batch * items
+        weight = jnp.where(lax.broadcasted_iota(jnp.int32, mod_own.shape, 0) == 6, 0.5, 1.0)
+        mod_all[first_row + z] = (mod_own[...] + mod_in[...]) * weight
+        mod_copies = []
+        for step in range(1, items):
+            place = mod_all.at[first_row + z]
+            there = at(y, x, (z + step) % items, core)
+            mod_copies.append(remote(place, place, m_send.at[step], m_recv.at[step], there))
+        sent.extend(mod_copies)
+        yield
+        for copy in mod_copies:
+            copy.wait_recv()
+        mod_copies = []
+        for index, device in enumerate((x_peer, y_peer, xy_peer)):
+            place = mod_all.at[pl.ds(first_row, items)]
+            slot = items + index
+            mod_copies.append(remote(place, place, m_send.at[slot], m_recv.at[slot], device))
+        sent.extend(mod_copies)
+        yield
+        for copy in mod_copies:
+            copy.wait_recv()
+        put(mod_all, out_mod)
+        yield
+        give_back(out_block, 0)
+        give_back(out_input, 1)
+
+    steps = compute()
+    streams = [stream(index, *what) for index, what in enumerate(STREAMS)]
+    for step in ORDER:
+        next(steps if step < 0 else streams[step], None)
+    for rest in [steps] + streams:
+        for _ in rest:
+            raise AssertionError
+
+    for copy in x_copies + g_copies + forwards + list(core_copies.values()) + sent:
+        copy.wait_send()
+    for copy in outs + puts:
+        copy.wait()
+
+
+def widen_kernel(
+    mod_in,
+    block_in_,
+    input_in,
+    fc2_in,
+    fc1_in,
+    qkvp_in,
+    block_out,
+    input_out,
+    ada_out,
+    bias_out,
+    qkv_out,
+    proj_out,
+    fc1_out,
+    fc2_out,
+    block_16,
+    input_16,
+    fc2_16,
+    fc1_16,
+    qkvp_16,
+    mod,
+    block_32,
+    input_32,
+    ada_32,
+    bias_32,
+    qkvp_32,
+    fc1_32,
+    fc2_32,
+    by_piece,
+    in_sem,
+    out_sem,
+):
+    width = fc1_in.shape[0]
+    pairs = (
+        (fc2_in, fc2_16),
+        (fc1_in, fc1_16),
+        (qkvp_in, qkvp_16),
+        (block_in_, block_16),
+        (input_in, input_16),
+    )
+    rows_load = pltpu.make_async_copy(mod_in, mod, in_sem.at[5])
+    rows_load.start()
+    loads = []
+    for index, (src, dst) in enumerate(pairs):
+        copy = pltpu.make_async_copy(src, dst, in_sem.at[index])
+        copy.start()
+        loads.append(copy)
+    stores = []
+
+    def store(src, dst):
+        copy = pltpu.make_async_copy(src, dst, out_sem.at[len(stores)])
+        copy.start()
+        stores.append(copy)
+
+    rows_load.wait()
+    count = mod.shape[0] // 8
+    for piece in range(7):
+        for item in range(count):
+            by_piece[piece, item : item + 1, :] = mod[item * 8 + piece : item * 8 + piece + 1, :]
+    conditions = jnp.concatenate([by_piece[6].astype(B16)] * 3, axis=0)
+    for piece in range(6):
+        columns = slice(piece * width, (piece + 1) * width)
+        rows = by_piece[piece]
+        bias_32[columns] = jnp.sum(rows, axis=0)
+        high = rows.astype(B16)
+        rest = rows - high.astype(F32)
+        middle = rest.astype(B16)
+        low = (rest - middle.astype(F32)).astype(B16)
+        parts = jnp.concatenate([high, middle, low], axis=0)
+        ada_32[:, columns] = dot(conditions, parts, TN)
+        store(ada_32.at[:, pl.ds(piece * width, width)], ada_out.at[:, pl.ds(piece * width, width)])
+    store(bias_32, bias_out)
+    loads[0].wait()
+    fc2_32[...] = fc2_16[...].astype(F32)
+    store(fc2_32, fc2_out)
+    loads[1].wait()
+    fc1_32[...] = fc1_16[...].astype(F32)
+    store(fc1_32, fc1_out)
+    loads[2].wait()
+    qkvp_32[...] = qkvp_16[...].astype(F32)
+    store(qkvp_32.at[:, pl.ds(0, 3 * width)], qkv_out)
+    store(qkvp_32.at[:, pl.ds(3 * width, width)], proj_out)
+    loads[3].wait()
+    block_32[...] = block_16[...].astype(F32)
+    store(block_32, block_out)
+    loads[4].wait()
+    input_32[...] = input_16[...].astype(F32)
+    store(input_32, input_out)
+    for copy in stores:
+        copy.wait()
+
+
+def widen(mod, out_block, out_input, fc2_sum, fc1_sum, qkvp_sum):
+    width, hidden = fc1_sum.shape
+    arrays = (out_block, out_input, fc2_sum, fc1_sum, qkvp_sum)
+    out_shapes = (
+        out_block.shape,
+        out_input.shape,
+        (width, 6 * width),
+        (6 * width,),
+        (width, 3 * width),
+        (width, width),
+        fc1_sum.shape,
+        fc2_sum.shape,
+    )
+    wide = (
+        out_block.shape,
+        out_input.shape,
+        (width, 6 * width),
+        (6 * width,),
+        qkvp_sum.shape,
+        fc1_sum.shape,
+        fc2_sum.shape,
+    )
+    hbm = pl.BlockSpec(memory_space=pl.ANY)
+    return pl.pallas_call(
+        widen_kernel,
+        out_shape=tuple(jax.ShapeDtypeStruct(shape, F32) for shape in out_shapes),
+        in_specs=[hbm] * 6,
+        out_specs=(hbm,) * 8,
+        scratch_shapes=[pltpu.VMEM(array.shape, B16) for array in arrays]
+        + [pltpu.VMEM(mod.shape, F32)]
+        + [pltpu.VMEM(shape, F32) for shape in wide]
+        + [pltpu.VMEM((7, mod.shape[0] // 8, width), F32)]
+        + [pltpu.SemaphoreType.DMA((6,)), pltpu.SemaphoreType.DMA((13,))],
+        name="widen",
+        compiler_params=pltpu.CompilerParams(vmem_limit_bytes=60 * 2**20),
+    )(mod, *arrays)
+
+
+def fused(block_in, lead_embed, lengths, w_ada, b_ada, w_qkv, w_proj, w_fc1, w_fc2, cotangent):
+    items, span, width = block_in.shape
+    hidden = w_fc1.shape[1]
+    groups = lax.axis_size("batch")
+    own = items * span
+    blocks = hidden // width
+    half = hidden // 2
+    waves = 3
+    hbm = pl.BlockSpec(memory_space=pl.ANY)
+    dma = pltpu.SemaphoreType.DMA
+    scratch = [
+        pltpu.SMEM(lengths.shape, jnp.int32),
+        pltpu.VMEM(lead_embed.shape, B16),
+        pltpu.VMEM(b_ada.shape, B16),
+        pltpu.VMEM(w_ada.shape, B16),
+        pltpu.VMEM(w_qkv.shape, B16),
+        pltpu.VMEM(w_proj.shape, B16),
+        pltpu.VMEM(w_fc1.shape, B16),
+        pltpu.VMEM(w_fc2.shape, B16),
+        pltpu.VMEM((2, items, span, width), B16),
+        pltpu.VMEM((items, span, width), B16),
+        pltpu.VMEM((1, 6 * width), F32),
+        pltpu.VMEM((2 * own, width), B16),
+        pltpu.VMEM((own, width), F32),
+        pltpu.VMEM((own, width), B16),
+        pltpu.VMEM((2 * own, 2 * width), B16),
+        pltpu.VMEM((2, 2 * own, 128), B16),
+        pltpu.VMEM((HEADS, 2 * own, own), B16),
+        pltpu.VMEM((8, own), F32),
+        pltpu.VMEM((own, width), B16),
+        pltpu.VMEM((own, width), F32),
+        pltpu.VMEM((own, width), F32),
+        pltpu.VMEM((blocks, own, width), B16),
+        pltpu.VMEM((blocks, own, width), F32),
+        pltpu.VMEM((blocks, own, width), B16),
+        pltpu.VMEM((3, own, width), B16),
+        pltpu.VMEM((2, items, span, width), B16),
+        pltpu.VMEM((own, width), F32),
+        pltpu.VMEM((own, width), F32),
+        pltpu.VMEM((blocks, width, width), F32),
+        pltpu.VMEM((waves, half, width), B16),
+        pltpu.VMEM((waves, half, width), B16),
+        pltpu.VMEM((waves, half, width), F32),
+        pltpu.VMEM((waves, half, width), B16),
+        pltpu.VMEM((waves, half, width), B16),
+        pltpu.VMEM((waves, hidden, width), B16),
+        pltpu.VMEM((8, width), F32),
+        pltpu.VMEM((8, width), F32),
+        pltpu.VMEM((groups * items, 8, width), F32),
+        dma((10,)),
+        dma((3 + 6 * len(STREAMS),)),
+    ]
+    for count in (items - 1, items, items - 1, 2 * items, 1, items + 3, 4):
+        scratch += [dma((count,))] * 2
+    scratch += [dma((len(STREAMS), 13))] * 2
+    out_block, out_input, fc2_sum, fc1_sum, qkvp_sum, mod = pl.pallas_call(
+        fused_kernel,
+        out_shape=(
+            jax.ShapeDtypeStruct(block_in.shape, B16),
+            jax.ShapeDtypeStruct(block_in.shape, B16),
+            jax.ShapeDtypeStruct((hidden, width), B16),
+            jax.ShapeDtypeStruct((width, hidden), B16),
+            jax.ShapeDtypeStruct((width, 4 * width), B16),
+            jax.ShapeDtypeStruct((groups * items, 8, width), F32),
+        ),
+        in_specs=[hbm] * 10,
+        out_specs=(hbm,) * 6,
+        scratch_shapes=scratch,
+        name="fused_block",
+        compiler_params=pltpu.CompilerParams(
+            collective_id=0, has_side_effects=True, vmem_limit_bytes=56 * 2**20
+        ),
+    )(
+        lengths,
+        block_in,
+        cotangent,
+        lead_embed,
+        b_ada,
+        w_ada,
+        w_qkv,
+        w_proj,
+        w_fc1,
+        w_fc2,
+    )
+    return widen(
+        mod.reshape(groups * items * 8, width), out_block, out_input, fc2_sum, fc1_sum, qkvp_sum
+    )
+
+
+def choose(*arrays):
+    items, span, width = arrays[0].shape
+    fits = (
+        lax.axis_size("batch") == 4
+        and items == 4
+        and lax.axis_size("wide") == 2 * items
+        and span == 64
+        and width == HEADS * HEAD_DIM == 384
+        and arrays[7].shape[1] == 4 * width
+    )
+    return (fused if fits else on_device)(*arrays)
+
+
 def solution(mesh):
     return jax.shard_map(
-        on_device,
+        choose,
         mesh=mesh,
         in_specs=(
             P("batch", "wide", None),

time: 538 us -> 71.6 us (0.13); the launches traced: 529 us -> 70.9 us
  waiting for transfers between devices: 230 us -> 0 us
  local copies, waits for them, and re-layouts: 181 us -> 0 us
  Pallas kernels: 0 us -> 70.1 us
  blocking collectives: 39.2 us -> 0 us
  matrix products: 28.7 us -> 0 us
  starting transfers between devices: 21.8 us -> 0 us
  between operations: 15.4 us -> 0.81 us
  other arithmetic: 12.8 us -> 0 us
    psum x1 -> x0, waiting for transfers between devices: 178 us -> none  [on_device(): lax.psum((ada_grad, bias_grad, qkv_grad, proj_grad, fc1_grad, fc2_grad),...]
    unnamed x116 -> x0, local copies, waits for them, and re-layouts: 77.8 us -> none
    pallas_call x0 -> x2, Pallas kernels: none -> 70.1 us  [the longest x1 64.5 us: fused(): pl.pallas_call(fused_kernel, out_shape=(jax.ShapeDtypeStruct(block_in.sha...]
    all_to_all x5 -> x0, waiting for transfers between devices: 52.2 us -> none  [the longest x1 16.9 us: on_device(): lax.all_to_all(to_heads(triple, 3, head_count, head_size), 'wide', split_...]
    all_to_all x7 -> x0, local copies, waits for them, and re-layouts: 48.6 us -> none  [the longest x1 42.2 us: on_device(): lax.all_to_all(triple_grad.reshape(3, pair_count, slot_len * head_size),...]
    psum x1 -> x0, blocking collectives: 39.2 us -> none  [on_device(): lax.psum((ada_grad, bias_grad, qkv_grad, proj_grad, fc1_grad, fc2_grad),...]
    another operation x8 -> x0, local copies, waits for them, and re-layouts: 35.2 us -> none  [the longest x4 34.2 us: attend_backward(): jnp.stack([join_rows(query_grads), key_grad, value_grad])]
    dot_general x22 -> x0, matrix products: 28.7 us -> none  [the longest x2 3.58 us: masked_scores(): jnp.einsum('pqd,pkd->pqk', query_block, keys_all, preferred_element_type=...]
  transfers between devices with their start and end apart: 6 -> 0, of which waited for: 6 -> 0; matrix products, arithmetic and copies ran while one was open for 5% -> 0% of each run, Pallas kernels for 0% -> 0%
where the time goes in v2:
time: 71.6 us; the launch traced here: 70.9 us
  Pallas kernels  70.1 us (98%)
  between operations  0.81 us (1%)
    pallas_call x1, Pallas kernels, fused(): pl.pallas_call(fused_kernel, out_shape=(jax.ShapeDtypeStruct(block_in.sha...  64.5 us
    pallas_call x1, Pallas kernels, widen(): pl.pallas_call(widen_kernel, out_shape=tuple((jax.ShapeDtypeStruct(shape,...  5.64 us

profile of v2, /device:TPU:0, one launch (start us, length us, event | category | flops | bytes accessed | tf_op | source)
XLA Modules:
  0.0 70.9 jit_solution(3981197548041057309)
XLA Ops:
  0.6 64.5 %fused_block.1 = (bf16[4,64,384]{2,1,0:T(8,128)(2,1)}, bf16[4,64,384]{2,1,0:T(8,128)(2,1)}, bf16[1536,384]{1,0:T(8,128)(2,1)}, bf16[384,1536]{1,0:T(8,128)(2,1)}...) custom-call(s32[4]{0:T(128)} %lengths_in.1, bf16[4,64,384]{2,1,0:T(8,128)(2,1)} %block_in.1, ...), custom_call_target="tpu_custom_call" | custom-call | tf_op jit(solution)/shard_map/fused_block/pallas_call | solution.py:1113
  65.1 5.6 %widen.1 = (f32[4,64,384]{2,1,0:T(8,128)}, f32[4,64,384]{2,1,0:T(8,128)}, f32[384,2304]{1,0:T(8,128)}, f32[2304]{0:T(1024)}, f32[384,1152]{1,0:T(8,128)}, /*inde...) custom-call(f32[128,384]{1,0:T(8,128)} %bitcast.1, bf16[4,64,384]{2,1,0:T(8,128)(2,1)} %get-tuple-element.15.block_in_, ...), custom_call_target="tpu_custom_call" | custom-call | tf_op jit(solution)/shard_map/widen/pallas_call | solution.py:1043

commit v3 on v2

--- a/solution.py
+++ b/solution.py
@@ -269,22 +269,28 @@
     (0, 256, 128, "pqzZ"),
     (0, 384, 256, "pqzZ"),
     (0, 640, 128, "pzZq"),
-    (1, 0, 256, "D"),
+    (1, 0, 256, "XW"),
     (1, 256, 256, "pqzZ"),
     (1, 512, 256, "zpqZ"),
-    (2, 0, 256, "pqzZ"),
+    (2, 0, 256, "pqzZ*"),
     (2, 256, 128, "pzqZ"),
-    (2, 384, 256, "pqzZ"),
-    (2, 640, 128, "zpqZ"),
+    (2, 384, 256, "pqzZ*"),
+    (2, 640, 128, "zpqZ*"),
 )
 ORDER = (
     -1, -1, -1, -1, -1, -1, -1, -1, 0, 1, 2, 3, -1, -1, -1, 4, 5, 6, -1, 1,
-    7, 8, 3, 0, 2, -1, -1, 4, 6, 3, 9, 10, 1, -1, 8, 0, 2, -1, 5, 4,
-    1, 7, 6, 3, 9, 10, 0, 8, -1, 2, 5, 3, 6, 4, 7, 1, 8, 10, 9, 0,
-    5, -1, 2, 3, 1, 10, 7, 6, 8, 4, 9, 0, 2, 5, 3, 4, 1, 6, 8, 10,
-    0, 7, 2, 5, 9, 3, 8, 10, 1, 6, 3, 1, 7, 5, 9, 10, 2, 8, -1, 0,
-    2, 8, 7, 0, 6, 9, 5, 6, 5, 7, 10, 9, 7, 10, 9,
+    7, 8, 3, 0, 2, -1, -1, 6, 4, 3, 9, 10, 1, -1, 8, 0, 2, 5, -1, 6,
+    7, 4, 1, 3, 9, 0, 10, 5, 8, 2, 6, -1, 7, 3, 9, 10, 8, 4, 1, 5,
+    -1, 0, 10, 3, 7, 1, 9, 2, 6, 8, 4, 0, 5, 10, 4, 1, 3, 6, 8, 7,
+    2, 0, 9, 5, 10, 1, 8, 3, 6, 7, 2, 1, 5, 3, 9, 8, -1, 10, 8, 0,
+    10, 0, 6, 7, 6, 9, 7, 2, 5, 9, 2, 5,
 )
+
+
+def copies_in(dims):
+    steps = dims.rstrip("*")
+    back = len(steps) - (steps[-1] not in "XW") - (dims[-1] == "*")
+    return len(steps) + back + 1
 
 
 def dot(left, right, dims):
@@ -308,10 +314,8 @@
     w_fc2_in,
     out_block,
     out_input,
-    out_fc2,
-    out_fc1,
-    out_qkvp,
-    out_mod,
+    total,
+    mod_all,
     lengths,
     lead_embed,
     b_ada,
@@ -346,27 +350,13 @@
     hold,
     stage,
     stage_in,
-    total,
     mod_own,
     mod_in,
-    mod_all,
     load_sem,
-    put_sem,
-    x_send,
+    send_sem,
     x_recv,
-    f_send,
-    f_recv,
-    g_send,
-    g_recv,
-    o_send,
-    o_recv,
-    e_send,
-    e_recv,
-    m_send,
-    m_recv,
-    c_send,
+    group_recv,
     c_recv,
-    s_send,
     s_recv,
 ):
     items, span, width = block_in.shape
@@ -401,11 +391,14 @@
         "Z": z // 2,
     }
 
-    def remote(src, dst, send, recv, device):
+    sent_rows = {}
+
+    def remote(src, dst, send, rows, recv, device):
+        sent_rows[send] = sent_rows.get(send, 0) + rows
         copy = pltpu.make_async_remote_copy(
             src_ref=src,
             dst_ref=dst,
-            send_sem=send,
+            send_sem=send_sem.at[send],
             recv_sem=recv,
             device_id=device,
             device_id_type=MESH,
@@ -418,12 +411,10 @@
         copy.start()
         return copy
 
-    puts = []
-
-    def put(src, dst):
-        copy = pltpu.make_async_copy(src, dst, put_sem.at[len(puts)])
-        copy.start()
-        puts.append(copy)
+    def wait_rows(sem, rows):
+        planes = next(p for p in (1, 2, 3) if rows % (16 * p) == 0 and rows <= p * total.shape[1])
+        area = total.at[pl.ds(0, planes), pl.ds(0, rows // planes)]
+        pltpu.make_async_copy(area, area, sem).wait()
 
     barrier = pltpu.get_barrier_semaphore()
     greet = [core_peer, x_peer, y_peer, xy_peer]
@@ -444,21 +435,20 @@
     ]
     pl.semaphore_wait(barrier, len(greet))
 
-    x_copies, g_copies = [], []
+    x_copies = []
     for step in range(1, items):
         there = (z + step) % items
         x_copies.append(
             remote(
                 block_in.at[there],
                 xall.at[0, z],
-                x_send.at[step - 1],
+                0,
+                span,
                 x_recv.at[step - 1],
                 at(y, x, there, core),
             )
         )
-    forwards = [
-        remote(block_in.at[z], xall.at[1, z], f_send.at[0], f_recv.at[0], core_peer)
-    ]
+    remote(block_in.at[z], xall.at[1, z], 0, span, group_recv.at[0], core_peer)
 
     for index in (7, 8, 9):
         loads[index].wait()
@@ -491,25 +481,23 @@
     for step in range(1, items):
         came = (z + items - step) % items
         x_copies[step - 1].wait_recv()
-        forwards.append(
-            remote(
-                xall.at[0, came],
-                xall.at[1, came],
-                f_send.at[step],
-                f_recv.at[step],
-                core_peer,
-            )
+        remote(
+            xall.at[0, came],
+            xall.at[1, came],
+            0,
+            span,
+            group_recv.at[0],
+            core_peer,
         )
     for step in range(1, items):
         there = (z + step) % items
-        g_copies.append(
-            remote(
-                cotangent.at[there],
-                gall.at[z],
-                g_send.at[step - 1],
-                g_recv.at[step - 1],
-                at(y, x, there, core),
-            )
+        remote(
+            cotangent.at[there],
+            gall.at[z],
+            0,
+            span,
+            group_recv.at[1],
+            at(y, x, there, core),
         )
 
     loads[2].wait()
@@ -519,30 +507,37 @@
     entry[:own, :] = (normed * (1.0 + scale_att) + shift_att).astype(B16)
     q_all[...] = (dot(entry[:own, :], w_qkv[:, :width], MM).astype(B16) * inv_root).astype(B16)
     kv_all[:own, :] = dot(entry[:own, :], w_qkv[:, width:], MM).astype(B16)
-    for copy in forwards:
-        copy.wait_recv()
+    wait_rows(group_recv.at[0], own)
     other_normed, _ = norm_rows(xall[1].reshape(own, width).astype(F32))
     entry[own:, :] = (other_normed * (1.0 + scale_att) + shift_att).astype(B16)
     kv_all[own:, :] = dot(entry[own:, :], w_qkv[:, width:], MM).astype(B16)
 
-    for pair in range(head_pairs):
+    def head_scores(head):
+        pair, half = divmod(head, 2)
         lanes = slice(pair * 128, (pair + 1) * 128)
-        v_lanes = slice(width + pair * 128, width + (pair + 1) * 128)
-        keys, values, queries = kv_all[:, lanes], kv_all[:, v_lanes], q_all[:, lanes]
-        parts = []
-        for half in range(2):
-            head = pair * 2 + half
-            scores = dot(
-                keys * halves[half] + bias_keys[half], queries * halves[half] + marks[half], NT
+        return dot(
+            kv_all[:, lanes] * halves[half] + bias_keys[half],
+            q_all[:, lanes] * halves[half] + marks[half],
+            NT,
+        )
+
+    scores, parts = head_scores(0), []
+    for head in range(HEADS):
+        pair, half = divmod(head, 2)
+        following = head_scores(head + 1) if head + 1 < HEADS else None
+        exp_scores = jnp.exp(scores - jnp.max(scores, axis=0, keepdims=True))
+        inverse = 1.0 / jnp.sum(exp_scores, axis=0, keepdims=True)
+        inverses[head : head + 1, :] = inverse
+        weights = exp_scores.astype(B16)
+        probs[head] = weights
+        out = dot(kv_all[:, width + pair * 128 : width + (pair + 1) * 128], weights, TN)
+        parts.append(out[half * HEAD_DIM : (half + 1) * HEAD_DIM] * inverse)
+        if half == 1:
+            mixed[:, pair * 128 : (pair + 1) * 128] = (
+                jnp.concatenate(parts, axis=0).T.astype(B16)
             )
-            exp_scores = jnp.exp(scores - jnp.max(scores, axis=0, keepdims=True))
-            inverse = 1.0 / jnp.sum(exp_scores, axis=0, keepdims=True)
-            inverses[head : head + 1, :] = inverse
-            weights = exp_scores.astype(B16)
-            probs[head] = weights
-            out = dot(values, weights, TN)[half * HEAD_DIM : (half + 1) * HEAD_DIM] * inverse
-            parts.append(out)
-        mixed[:, lanes] = jnp.concatenate(parts, axis=0).T.astype(B16)
+            parts = []
+        scores = following
 
     loads[3].wait()
     branch = dot(mixed[...], w_proj[...], MM)
@@ -566,138 +561,46 @@
         )
         mlp_out = mlp_out + dot(act, w_fc2[columns, :], MM)
 
-    outs = []
-
     def give_back(out, which):
         for step in range(1, items):
             there = (z + step) % items
-            slot = which * items + step
-            outs.append(
-                remote(
-                    send_out.at[which, there],
-                    out.at[z],
-                    o_send.at[slot],
-                    o_recv.at[slot],
-                    at(y, x, there, core),
-                )
+            remote(
+                send_out.at[which, there],
+                out.at[z],
+                0,
+                span,
+                group_recv.at[2 + which],
+                at(y, x, there, core),
             )
-        put(send_out.at[which, z], out.at[z])
+        out[z] = send_out[which, z]
 
     def rows_of(start, count):
         return pl.ds(pl.multiple_of(start, 16), count)
 
+    first_slot = [sum(copies_in(what[3]) for what in STREAMS[:k]) for k in range(len(STREAMS))]
     core_copies = {}
     core_done = set()
-    sent = []
 
     def core_start(wave, first, count):
         rows = pl.ds(first, count)
         core_copies[wave, first] = remote(
             core_out.at[wave, rows],
             core_in.at[wave, rows],
-            c_send.at[len(core_copies)],
+            1 + wave,
+            count,
             c_recv.at[len(core_copies)],
             core_peer,
         )
 
-    def write_out(wave, at_core, base, count):
-        first = at_core * half_rows + base
-        if wave == 0:
-            rows = rows_of(first, count)
-            put(total.at[wave, rows, :], out_fc2.at[rows, :])
-            return
-        done = 0
-        while done < count:
-            block, inside = divmod(base + done, width)
-            size = min(count - done, width - inside)
-            rows, out_rows = rows_of(first + done, size), pl.ds(inside, size)
-            if wave == 1:
-                columns = pl.ds(pl.multiple_of((at_core * 2 + block) * width, 128), width)
-                put(total.at[wave, rows, :], out_fc1.at[out_rows, columns])
-            else:
-                if block == 0:
-                    start, stride = at_core * 3 * width, width - at_core * (width - 128)
-                else:
-                    start, stride = 128 + at_core * 128, width
-                for piece in range(3):
-                    columns = pl.ds(pl.multiple_of(start + piece * stride, 128), 128)
-                    put(
-                        total.at[wave, rows, pl.ds(piece * 128, 128)],
-                        out_qkvp.at[out_rows, columns],
-                    )
-            done += size
-
     groups = {
-        "xy": (y * 2 + x, ((y * 2 + 1 - x, x_peer), (2 - y * 2 + x, y_peer), (3 - y * 2 - x, xy_peer))),
-        "z": (
+        "X": (y * 2 + x, ((y * 2 + 1 - x, x_peer), (2 - y * 2 + x, y_peer), (3 - y * 2 - x, xy_peer))),
+        "W": (
             z,
             tuple(
                 ((z + step) % items, at(y, x, (z + step) % items, core)) for step in range(1, items)
             ),
         ),
     }
-
-    def direct(index, wave, base, count, order):
-        slot, kept, size, place = 0, base, count, base
-        before = core_in
-        places = []
-        for name in order:
-            side, others = groups[name]
-            size //= 4
-            copies = []
-            for number, (other, device) in reversed(list(enumerate(others))):
-                away = kept + other * size
-                area = pl.ds(place + number * size, size)
-                values = hold[wave, rows_of(away, size), :]
-                if before is not None:
-                    values = values + before[wave, rows_of(away, size), :].astype(F32)
-                stage[wave, area, :] = values.astype(B16)
-                copies.append(
-                    remote(
-                        stage.at[wave, area],
-                        stage_in.at[wave, area],
-                        s_send.at[index, slot],
-                        s_recv.at[index, slot],
-                        device,
-                    )
-                )
-                slot += 1
-            sent.extend(copies)
-            kept = kept + side * size
-            yield
-            for copy in copies:
-                copy.wait_recv()
-            values = hold[wave, rows_of(kept, size), :]
-            if before is not None:
-                values = values + before[wave, rows_of(kept, size), :].astype(F32)
-            for number in range(3):
-                area = pl.ds(place + number * size, size)
-                values = values + stage_in[wave, area, :].astype(F32)
-            if len(places) == 0:
-                hold[wave, rows_of(kept, size), :] = values
-            else:
-                total[wave, rows_of(core * half_rows + kept, size), :] = values.astype(B16)
-            places.append((others, kept, size))
-            before, place = None, place + 3 * size
-        for others, start, size in reversed(places):
-            area = total.at[wave, rows_of(core * half_rows + start, size)]
-            copies = []
-            for _, device in reversed(others):
-                copies.append(
-                    remote(area, area, s_send.at[index, slot], s_recv.at[index, slot], device)
-                )
-                slot += 1
-            sent.extend(copies)
-            yield
-            for copy in copies:
-                copy.wait_recv()
-        area = total.at[wave, rows_of(core * half_rows + base, count)]
-        copy = remote(area, area, s_send.at[index, slot], s_recv.at[index, slot], core_peer)
-        sent.append(copy)
-        write_out(wave, core, base, count)
-        yield
-        copy.wait_recv()
-        write_out(wave, 1 - core, base, count)
 
     def stream(index, wave, base, count, dims):
         keys = [first for kept_wave, first in core_copies if kept_wave == wave]
@@ -706,79 +609,95 @@
                 continue
             core_done.add((wave, key))
             core_copies[wave, key].wait_recv()
-        if dims in "DE":
-            yield from direct(index, wave, base, count, ("xy", "z") if dims == "D" else ("z", "xy"))
-            return
-        slot = 0
+        slot = first_slot[index]
         kept, size, place = base, count, base
-        before, before_at = core_in, base
-        places = []
-        for dim in dims[:-1]:
-            size //= 2
-            away, keep = (1 - sides[dim]) * size, sides[dim] * size
-            area = pl.ds(place, size)
-            stage[wave, area, :] = (
-                hold[wave, rows_of(kept + away, size), :]
-                + before[wave, rows_of(before_at + away, size), :].astype(F32)
-            ).astype(B16)
-            copy = remote(
+        terms, terms_at, terms_step, term_count = core_in, base, 0, 1
+        back = []
+
+        def summed(offset, rows):
+            values = hold[wave, rows_of(kept + offset, rows), :]
+            for number in range(term_count):
+                area = rows_of(terms_at + number * terms_step + offset, rows)
+                values = values + terms[wave, area, :].astype(F32)
+            return values
+
+        def send(area, device):
+            return remote(
                 stage.at[wave, area],
                 stage_in.at[wave, area],
-                s_send.at[index, slot],
-                s_recv.at[index, slot],
-                peers[dim],
+                4 + index,
+                area.size,
+                s_recv.at[slot],
+                device,
             )
-            sent.append(copy)
-            hold[wave, rows_of(kept + keep, size), :] += before[
-                wave, rows_of(before_at + keep, size), :
-            ].astype(F32)
-            places.append((dim, kept + keep, size))
-            kept, slot = kept + keep, slot + 1
-            before, before_at, place = stage_in, place, place + size
+
+        result = None
+        steps = dims.rstrip("*")
+        for number, dim in enumerate(steps):
+            last = number == len(steps) - 1
+            if dim in groups:
+                side, others = groups[dim]
+                size //= 4
+                for other_number, (other, device) in reversed(list(enumerate(others))):
+                    area = pl.ds(place + other_number * size, size)
+                    stage[wave, area, :] = summed(other * size, size).astype(B16)
+                    send(area, device)
+                mine = summed(side * size, size)
+                hold[wave, rows_of(kept + side * size, size), :] = mine
+                kept = kept + side * size
+                back.append((dim, kept, size))
+                terms, terms_at, terms_step, term_count = stage_in, place, size, 3
+                place = place + 3 * size
+            elif not last:
+                size //= 2
+                away, keep = (1 - sides[dim]) * size, sides[dim] * size
+                area = pl.ds(place, size)
+                stage[wave, area, :] = summed(away, size).astype(B16)
+                send(area, peers[dim])
+                mine = summed(keep, size)
+                hold[wave, rows_of(kept + keep, size), :] = mine
+                kept = kept + keep
+                back.append((dim, kept, size))
+                terms, terms_at, terms_step, term_count = stage_in, place, 0, 1
+                place = place + size
+            else:
+                area = pl.ds(place, size)
+                stage[wave, area, :] = summed(0, size).astype(B16)
+                send(area, peers[dim])
+                result = area
             yield
-            copy.wait_recv()
-        area = pl.ds(place, size)
-        stage[wave, area, :] = (
-            hold[wave, rows_of(kept, size), :]
-            + before[wave, rows_of(before_at, size), :].astype(F32)
-        ).astype(B16)
-        copy = remote(
-            stage.at[wave, area],
-            stage_in.at[wave, area],
-            s_send.at[index, slot],
-            s_recv.at[index, slot],
-            peers[dims[-1]],
-        )
-        sent.append(copy)
-        slot += 1
+            wait_rows(s_recv.at[slot], 3 * size if dim in groups else size)
+            slot += 1
+        if result is None:
+            values = summed(0, size)
+        else:
+            values = stage[wave, result, :].astype(F32) + stage_in[wave, result, :].astype(F32)
+        total[wave, rows_of(core * half_rows + kept, size), :] = values.astype(B16)
+
+        back.reverse()
+        while back:
+            dim, start, size = back.pop(0)
+            if dims.endswith("*") and dim in "pq" and back and back[0][0] in "pq":
+                back.pop(0)
+                dim = "X"
+            area = total.at[wave, rows_of(core * half_rows + start, size)]
+            devices = [device for _, device in reversed(groups[dim][1])] if dim in groups else [peers[dim]]
+            for device in devices:
+                remote(area, area, 4 + index, size, s_recv.at[slot], device)
+            yield
+            wait_rows(s_recv.at[slot], len(devices) * size)
+            slot += 1
+        area = total.at[wave, rows_of(core * half_rows + base, count)]
+        copy = remote(area, area, 4 + index, count, s_recv.at[slot], core_peer)
         yield
         copy.wait_recv()
-        here = core * half_rows
-        total[wave, rows_of(here + kept, size), :] = (
-            stage[wave, area, :].astype(F32) + stage_in[wave, area, :].astype(F32)
-        ).astype(B16)
-        for dim, start, size in reversed(places):
-            area = total.at[wave, rows_of(here + start, size)]
-            copy = remote(area, area, s_send.at[index, slot], s_recv.at[index, slot], peers[dim])
-            sent.append(copy)
-            slot += 1
-            yield
-            copy.wait_recv()
-        area = total.at[wave, rows_of(here + base, count)]
-        copy = remote(area, area, s_send.at[index, slot], s_recv.at[index, slot], core_peer)
-        sent.append(copy)
-        write_out(wave, core, base, count)
-        yield
-        copy.wait_recv()
-        write_out(wave, 1 - core, base, count)
 
     def compute():
         per_core = blocks // 2
         block_result = middle + gate_mlp * mlp_out
         send_out[0] = block_result.astype(B16).reshape(items, span, width)
         loads[6].wait()
-        for copy in g_copies:
-            copy.wait_recv()
+        wait_rows(group_recv.at[1], own - span)
         gradient = gall[...].reshape(own, width).astype(F32)
         mlp_grad = (gate_mlp * gradient).astype(B16)
         grads_bf[1] = mlp_grad
@@ -868,8 +787,7 @@
             yield
 
         entry_send[...] = dot(dkv[own:, :], w_qkv[:, width:], NT)
-        entry_copy = remote(entry_send, entry_recv, e_send.at[0], e_recv.at[0], core_peer)
-        sent.append(entry_copy)
+        entry_copy = remote(entry_send, entry_recv, 0, 2 * own, group_recv.at[4], core_peer)
         entry_grad = dot(dkv[:own, :], w_qkv[:, width:], NT) + dot(dq[...], w_qkv[:, :width], NT)
         yield
         entry_copy.wait_recv()
@@ -877,8 +795,7 @@
         normed = normed_own[...]
         mod_own[1:2, :] = col_sum(entry_grad * normed)
         mod_own[0:1, :] = col_sum(entry_grad)
-        mod_copy = remote(mod_own, mod_in, m_send.at[0], m_recv.at[0], core_peer)
-        sent.append(mod_copy)
+        mod_copy = remote(mod_own, mod_in, 0, 16, group_recv.at[5], core_peer)
         input_grad = middle_grad + norm_back(
             normed, norm_inverse, entry_grad * (1.0 + scale_att)
         )
@@ -888,25 +805,17 @@
         first_row = batch * items
         weight = jnp.where(lax.broadcasted_iota(jnp.int32, mod_own.shape, 0) == 6, 0.5, 1.0)
         mod_all[first_row + z] = (mod_own[...] + mod_in[...]) * weight
-        mod_copies = []
         for step in range(1, items):
             place = mod_all.at[first_row + z]
             there = at(y, x, (z + step) % items, core)
-            mod_copies.append(remote(place, place, m_send.at[step], m_recv.at[step], there))
-        sent.extend(mod_copies)
-        yield
-        for copy in mod_copies:
-            copy.wait_recv()
-        mod_copies = []
-        for index, device in enumerate((x_peer, y_peer, xy_peer)):
+            remote(place, place, 0, 16, group_recv.at[6], there)
+        yield
+        wait_rows(group_recv.at[6], 16 * (items - 1))
+        for device in (x_peer, y_peer, xy_peer):
             place = mod_all.at[pl.ds(first_row, items)]
-            slot = items + index
-            mod_copies.append(remote(place, place, m_send.at[slot], m_recv.at[slot], device))
-        sent.extend(mod_copies)
-        yield
-        for copy in mod_copies:
-            copy.wait_recv()
-        put(mod_all, out_mod)
+            remote(place, place, 0, 16 * items, group_recv.at[7], device)
+        yield
+        wait_rows(group_recv.at[7], 3 * 16 * items)
         yield
         give_back(out_block, 0)
         give_back(out_input, 1)
@@ -919,19 +828,17 @@
         for _ in rest:
             raise AssertionError
 
-    for copy in x_copies + g_copies + forwards + list(core_copies.values()) + sent:
-        copy.wait_send()
-    for copy in outs + puts:
-        copy.wait()
+    for which in range(2):
+        wait_rows(group_recv.at[2 + which], own - span)
+    for index, rows in sent_rows.items():
+        wait_rows(send_sem.at[index], rows)
 
 
 def widen_kernel(
-    mod_in,
-    block_in_,
-    input_in,
-    fc2_in,
-    fc1_in,
-    qkvp_in,
+    block_16,
+    input_16,
+    total,
+    mod,
     block_out,
     input_out,
     ada_out,
@@ -940,50 +847,35 @@
     proj_out,
     fc1_out,
     fc2_out,
-    block_16,
-    input_16,
-    fc2_16,
-    fc1_16,
-    qkvp_16,
-    mod,
     block_32,
     input_32,
     ada_32,
     bias_32,
-    qkvp_32,
+    qkv_32,
+    proj_32,
     fc1_32,
     fc2_32,
     by_piece,
-    in_sem,
-    out_sem,
+    sem,
 ):
-    width = fc1_in.shape[0]
-    pairs = (
-        (fc2_in, fc2_16),
-        (fc1_in, fc1_16),
-        (qkvp_in, qkvp_16),
-        (block_in_, block_16),
-        (input_in, input_16),
-    )
-    rows_load = pltpu.make_async_copy(mod_in, mod, in_sem.at[5])
-    rows_load.start()
-    loads = []
-    for index, (src, dst) in enumerate(pairs):
-        copy = pltpu.make_async_copy(src, dst, in_sem.at[index])
-        copy.start()
-        loads.append(copy)
+    count, _, width = mod.shape
+    blocks = fc2_32.shape[0] // width
     stores = []
 
     def store(src, dst):
-        copy = pltpu.make_async_copy(src, dst, out_sem.at[len(stores)])
+        copy = pltpu.make_async_copy(src, dst, sem.at[len(stores)])
         copy.start()
         stores.append(copy)
 
-    rows_load.wait()
-    count = mod.shape[0] // 8
+    def part(index):
+        return pl.ds(index * width, width)
+
+    for block in range(blocks):
+        fc2_32[part(block), :] = total[0, part(block), :].astype(F32)
+        store(fc2_32.at[part(block), :], fc2_out.at[part(block), :])
     for piece in range(7):
         for item in range(count):
-            by_piece[piece, item : item + 1, :] = mod[item * 8 + piece : item * 8 + piece + 1, :]
+            by_piece[piece, item : item + 1, :] = mod[item, piece : piece + 1, :]
     conditions = jnp.concatenate([by_piece[6].astype(B16)] * 3, axis=0)
     for piece in range(6):
         columns = slice(piece * width, (piece + 1) * width)
@@ -995,64 +887,54 @@
         low = (rest - middle.astype(F32)).astype(B16)
         parts = jnp.concatenate([high, middle, low], axis=0)
         ada_32[:, columns] = dot(conditions, parts, TN)
-        store(ada_32.at[:, pl.ds(piece * width, width)], ada_out.at[:, pl.ds(piece * width, width)])
+        store(ada_32.at[:, part(piece)], ada_out.at[:, part(piece)])
     store(bias_32, bias_out)
-    loads[0].wait()
-    fc2_32[...] = fc2_16[...].astype(F32)
-    store(fc2_32, fc2_out)
-    loads[1].wait()
-    fc1_32[...] = fc1_16[...].astype(F32)
-    store(fc1_32, fc1_out)
-    loads[2].wait()
-    qkvp_32[...] = qkvp_16[...].astype(F32)
-    store(qkvp_32.at[:, pl.ds(0, 3 * width)], qkv_out)
-    store(qkvp_32.at[:, pl.ds(3 * width, width)], proj_out)
-    loads[3].wait()
+    for block in range(blocks):
+        columns = slice(block * width, (block + 1) * width)
+        fc1_32[:, columns] = total[1, part(block), :].astype(F32)
+        store(fc1_32.at[:, part(block)], fc1_out.at[:, part(block)])
+    proj_32[...] = total[2, part(2), :].astype(F32)
+    store(proj_32, proj_out)
+    for pair, block in enumerate((0, 1, 3)):
+        for piece in range(3):
+            start = piece * width + pair * 128
+            qkv_32[:, start : start + 128] = total[
+                2, part(block), piece * 128 : (piece + 1) * 128
+            ].astype(F32)
+    store(qkv_32, qkv_out)
     block_32[...] = block_16[...].astype(F32)
     store(block_32, block_out)
-    loads[4].wait()
     input_32[...] = input_16[...].astype(F32)
     store(input_32, input_out)
     for copy in stores:
         copy.wait()
 
 
-def widen(mod, out_block, out_input, fc2_sum, fc1_sum, qkvp_sum):
-    width, hidden = fc1_sum.shape
-    arrays = (out_block, out_input, fc2_sum, fc1_sum, qkvp_sum)
-    out_shapes = (
+def widen(out_block, out_input, total, mod):
+    waves, hidden, width = total.shape
+    shapes = (
         out_block.shape,
         out_input.shape,
         (width, 6 * width),
         (6 * width,),
         (width, 3 * width),
         (width, width),
-        fc1_sum.shape,
-        fc2_sum.shape,
-    )
-    wide = (
-        out_block.shape,
-        out_input.shape,
-        (width, 6 * width),
-        (6 * width,),
-        qkvp_sum.shape,
-        fc1_sum.shape,
-        fc2_sum.shape,
-    )
-    hbm = pl.BlockSpec(memory_space=pl.ANY)
+        (width, hidden),
+        (hidden, width),
+    )
     return pl.pallas_call(
         widen_kernel,
-        out_shape=tuple(jax.ShapeDtypeStruct(shape, F32) for shape in out_shapes),
-        in_specs=[hbm] * 6,
-        out_specs=(hbm,) * 8,
-        scratch_shapes=[pltpu.VMEM(array.shape, B16) for array in arrays]
-        + [pltpu.VMEM(mod.shape, F32)]
-        + [pltpu.VMEM(shape, F32) for shape in wide]
-        + [pltpu.VMEM((7, mod.shape[0] // 8, width), F32)]
-        + [pltpu.SemaphoreType.DMA((6,)), pltpu.SemaphoreType.DMA((13,))],
+        out_shape=tuple(jax.ShapeDtypeStruct(shape, F32) for shape in shapes),
+        in_specs=[pl.BlockSpec(memory_space=pltpu.VMEM)] * 4,
+        out_specs=(pl.BlockSpec(memory_space=pl.ANY),) * 8,
+        scratch_shapes=[pltpu.VMEM(shape, F32) for shape in shapes]
+        + [
+            pltpu.VMEM((7, mod.shape[0], width), F32),
+            pltpu.SemaphoreType.DMA((11 + 2 * (hidden // width),)),
+        ],
         name="widen",
-        compiler_params=pltpu.CompilerParams(vmem_limit_bytes=60 * 2**20),
-    )(mod, *arrays)
+        compiler_params=pltpu.CompilerParams(vmem_limit_bytes=30 * 2**20),
+    )(out_block, out_input, total, mod)
 
 
 def fused(block_in, lead_embed, lengths, w_ada, b_ada, w_qkv, w_proj, w_fc1, w_fc2, cotangent):
@@ -1100,32 +982,29 @@
         pltpu.VMEM((waves, half, width), F32),
         pltpu.VMEM((waves, half, width), B16),
         pltpu.VMEM((waves, half, width), B16),
-        pltpu.VMEM((waves, hidden, width), B16),
         pltpu.VMEM((8, width), F32),
         pltpu.VMEM((8, width), F32),
-        pltpu.VMEM((groups * items, 8, width), F32),
         dma((10,)),
-        dma((3 + 6 * len(STREAMS),)),
+        dma((4 + len(STREAMS),)),
+        dma((items - 1,)),
+        dma((8,)),
+        dma((4,)),
+        dma((sum(copies_in(what[3]) for what in STREAMS),)),
     ]
-    for count in (items - 1, items, items - 1, 2 * items, 1, items + 3, 4):
-        scratch += [dma((count,))] * 2
-    scratch += [dma((len(STREAMS), 13))] * 2
-    out_block, out_input, fc2_sum, fc1_sum, qkvp_sum, mod = pl.pallas_call(
+    results = pl.pallas_call(
         fused_kernel,
         out_shape=(
-            jax.ShapeDtypeStruct(block_in.shape, B16),
-            jax.ShapeDtypeStruct(block_in.shape, B16),
-            jax.ShapeDtypeStruct((hidden, width), B16),
-            jax.ShapeDtypeStruct((width, hidden), B16),
-            jax.ShapeDtypeStruct((width, 4 * width), B16),
-            jax.ShapeDtypeStruct((groups * items, 8, width), F32),
+            pltpu.VMEM(block_in.shape, B16),
+            pltpu.VMEM(block_in.shape, B16),
+            pltpu.VMEM((waves, hidden, width), B16),
+            pltpu.VMEM((groups * items, 8, width), F32),
         ),
         in_specs=[hbm] * 10,
-        out_specs=(hbm,) * 6,
+        out_specs=(pl.BlockSpec(memory_space=pltpu.VMEM),) * 4,
         scratch_shapes=scratch,
         name="fused_block",
         compiler_params=pltpu.CompilerParams(
-            collective_id=0, has_side_effects=True, vmem_limit_bytes=56 * 2**20
+            collective_id=0, has_side_effects=True, vmem_limit_bytes=58 * 2**20
         ),
     )(
         lengths,
@@ -1139,9 +1018,7 @@
         w_fc1,
         w_fc2,
     )
-    return widen(
-        mod.reshape(groups * items * 8, width), out_block, out_input, fc2_sum, fc1_sum, qkvp_sum
-    )
+    return widen(*results)
 
 
 def choose(*arrays):

time: 71.6 us -> 65.9 us (0.920)
  Pallas kernels: 70.1 us -> 64.9 us
    pallas_call x1, Pallas kernels: 64.5 us -> 60.3 us  [fused(): pl.pallas_call(fused_kernel, out_shape=(pltpu.VMEM(block_in.shape, B16),...]
    pallas_call x1, Pallas kernels: 5.64 us -> 4.65 us  [widen(): pl.pallas_call(widen_kernel, out_shape=tuple((jax.ShapeDtypeStruct(shape,...]
where the time goes in v3:
time: 65.9 us; the launch traced here: 65.7 us
  Pallas kernels  64.9 us (98%)
  between operations  0.81 us (1%)
    pallas_call x1, Pallas kernels, fused(): pl.pallas_call(fused_kernel, out_shape=(pltpu.VMEM(block_in.shape, B16),...  60.3 us
    pallas_call x1, Pallas kernels, widen(): pl.pallas_call(widen_kernel, out_shape=tuple((jax.ShapeDtypeStruct(shape,...  4.65 us

profile of v3, /device:TPU:0, one launch (start us, length us, event | category | flops | bytes accessed | tf_op | source)
XLA Modules:
  0.0 65.7 jit_solution(9823788443169753204)
XLA Ops:
  0.6 60.3 %fused_block.1 = (bf16[4,64,384]{2,1,0:T(8,128)(2,1)S(1)}, bf16[4,64,384]{2,1,0:T(8,128)(2,1)S(1)}, bf16[3,1536,384]{2,1,0:T(8,128)(2,1)S(1)}, f32[16,8,384]{2,1,0:T(8,128)S(1)}) custom-call(s32[4]{0:T(128)} %lengths_in.1, bf16[4,64,384]{2,1,0:T(8,128)(2,1)} %block_in.1, bf16[4,64,384]{2,1,0:T(8,128)(2,1)} %cotangent.1, bf16[4,384]{1,0:T(4,128)(2,1)} %lead_embed_in.1, ...), custom_call_target="tpu_custom_call" | custom-call | tf_op jit(solution)/shard_map/fused_block/pallas_call | solution.py:994
  60.9 4.6 %widen.1 = (f32[4,64,384]{2,1,0:T(8,128)}, f32[4,64,384]{2,1,0:T(8,128)}, f32[384,2304]{1,0:T(8,128)}, f32[2304]{0:T(1024)}, f32[384,1152]{1,0:T(8,128)}, /*inde...) custom-call(bf16[4,64,384]{2,1,0:T(8,128)(2,1)S(1)} %get-tuple-element.12.block_16, ...), custom_call_target="tpu_custom_call" | custom-call | tf_op jit(solution)/shard_map/widen/pallas_call | solution.py:925

commit v4 on v3

--- a/solution.py
+++ b/solution.py
@@ -274,16 +274,15 @@
     (1, 512, 256, "zpqZ"),
     (2, 0, 256, "pqzZ*"),
     (2, 256, 128, "pzqZ"),
-    (2, 384, 256, "pqzZ*"),
-    (2, 640, 128, "zpqZ*"),
+    (2, 384, 384, "pqzZ*"),
 )
 ORDER = (
-    -1, -1, -1, -1, -1, -1, -1, -1, 0, 1, 2, 3, -1, -1, -1, 4, 5, 6, -1, 1,
-    7, 8, 3, 0, 2, -1, -1, 6, 4, 3, 9, 10, 1, -1, 8, 0, 2, 5, -1, 6,
-    7, 4, 1, 3, 9, 0, 10, 5, 8, 2, 6, -1, 7, 3, 9, 10, 8, 4, 1, 5,
-    -1, 0, 10, 3, 7, 1, 9, 2, 6, 8, 4, 0, 5, 10, 4, 1, 3, 6, 8, 7,
-    2, 0, 9, 5, 10, 1, 8, 3, 6, 7, 2, 1, 5, 3, 9, 8, -1, 10, 8, 0,
-    10, 0, 6, 7, 6, 9, 7, 2, 5, 9, 2, 5,
+    -1, -1, -1, -1, -1, -1, -1, -1, 0, 1, 2, 3, -1, -1, 4, 5, 6, -1, -1, -1,
+    1, -1, -1, 0, 7, 8, 3, -1, 6, -1, 4, 1, 2, 9, 3, -1, 0, 5, 8, 6,
+    1, 7, 4, 2, 3, -1, 0, 8, 5, 6, 1, 9, 7, 3, 8, 4, 2, -1, 0, 5,
+    1, 9, 6, 7, 3, 8, 2, 0, 5, 9, 1, 3, 7, 4, 8, 6, 2, 0, 5, 4,
+    1, 3, -1, 7, 9, 8, 1, 6, 3, 2, 5, 0, -1, 9, 0, 7, 8, 7, 8, 2,
+    6, 5, 9, 2, 6, 5, 9,
 )
 
 
@@ -340,7 +339,11 @@
     active,
     gelu_slope,
     hidden_grad,
-    grads_bf,
+    mixed_grad,
+    entry_t,
+    second_t,
+    mixed_t,
+    keys_t,
     send_out,
     entry_send,
     entry_recv,
@@ -546,7 +549,6 @@
     second_normed, second_inverse = norm_rows(middle)
     second_ref[...] = second_normed
     second = (second_normed * (1.0 + scale_mlp) + shift_mlp).astype(B16)
-    grads_bf[0] = second
     loads[4].wait()
     loads[5].wait()
     mlp_out = jnp.zeros((own, width), F32)
@@ -555,11 +557,16 @@
         hidden = dot(second, w_fc1[:, columns], MM)
         cumulative = 0.5 * (1.0 + lax.erf(hidden * (0.5**0.5)))
         act = (hidden * cumulative).astype(B16)
-        active[block] = act
+        active[block] = act.T
         gelu_slope[block] = cumulative + hidden * (
             jnp.exp(-0.5 * hidden * hidden) * (1.0 / math.sqrt(2.0 * math.pi))
         )
         mlp_out = mlp_out + dot(act, w_fc2[columns, :], MM)
+
+    entry_t[...] = entry[...].T
+    second_t[...] = second.T
+    mixed_t[...] = mixed[...].T
+    keys_t[...] = kv_all[:, :width].T
 
     def give_back(out, which):
         for step in range(1, items):
@@ -611,14 +618,13 @@
             core_copies[wave, key].wait_recv()
         slot = first_slot[index]
         kept, size, place = base, count, base
-        terms, terms_at, terms_step, term_count = core_in, base, 0, 1
+        terms = [(core_in, base)]
         back = []
 
         def summed(offset, rows):
             values = hold[wave, rows_of(kept + offset, rows), :]
-            for number in range(term_count):
-                area = rows_of(terms_at + number * terms_step + offset, rows)
-                values = values + terms[wave, area, :].astype(F32)
+            for array, at_row in terms:
+                values = values + array[wave, rows_of(at_row + offset, rows), :].astype(F32)
             return values
 
         def send(area, device):
@@ -642,11 +648,10 @@
                     area = pl.ds(place + other_number * size, size)
                     stage[wave, area, :] = summed(other * size, size).astype(B16)
                     send(area, device)
-                mine = summed(side * size, size)
-                hold[wave, rows_of(kept + side * size, size), :] = mine
                 kept = kept + side * size
                 back.append((dim, kept, size))
-                terms, terms_at, terms_step, term_count = stage_in, place, size, 3
+                terms = [(array, at_row + side * size) for array, at_row in terms]
+                terms += [(stage_in, place + other_number * size) for other_number in range(3)]
                 place = place + 3 * size
             elif not last:
                 size //= 2
@@ -654,11 +659,9 @@
                 area = pl.ds(place, size)
                 stage[wave, area, :] = summed(away, size).astype(B16)
                 send(area, peers[dim])
-                mine = summed(keep, size)
-                hold[wave, rows_of(kept + keep, size), :] = mine
                 kept = kept + keep
                 back.append((dim, kept, size))
-                terms, terms_at, terms_step, term_count = stage_in, place, 0, 1
+                terms = [(array, at_row + keep) for array, at_row in terms] + [(stage_in, place)]
                 place = place + size
             else:
                 area = pl.ds(place, size)
@@ -700,17 +703,16 @@
         wait_rows(group_recv.at[1], own - span)
         gradient = gall[...].reshape(own, width).astype(F32)
         mlp_grad = (gate_mlp * gradient).astype(B16)
-        grads_bf[1] = mlp_grad
         for index in range(per_core):
             block = (1 - core) * per_core + index
             rows = slice(index * width, (index + 1) * width)
-            core_out[0, rows, :] = dot(active[block], mlp_grad, TN).astype(B16)
+            core_out[0, rows, :] = dot(active[block], mlp_grad, MM).astype(B16)
         core_start(0, 0, half_rows)
         yield
         for index in range(per_core):
             block = core * per_core + index
             rows = slice(index * width, (index + 1) * width)
-            hold[0, rows, :] = dot(active[block], mlp_grad, TN)
+            hold[0, rows, :] = dot(active[block], mlp_grad, MM)
         yield
         second_grad = jnp.zeros((own, width), F32)
         for block in range(blocks):
@@ -723,21 +725,21 @@
         for index in range(per_core):
             block = (1 - core) * per_core + index
             rows = slice(index * width, (index + 1) * width)
-            core_out[1, rows, :] = dot(grads_bf[0], hidden_grad[block], TN).astype(B16)
+            core_out[1, rows, :] = dot(second_t[...], hidden_grad[block], MM).astype(B16)
         core_start(1, 0, half_rows)
         yield
         for index in range(per_core):
             block = core * per_core + index
             rows = slice(index * width, (index + 1) * width)
-            hold[1, rows, :] = dot(grads_bf[0], hidden_grad[block], TN)
+            hold[1, rows, :] = dot(second_t[...], hidden_grad[block], MM)
         yield
         second_normed = second_ref[...]
         middle_grad = gradient + norm_back(
             second_normed, second_inverse, second_grad * (1.0 + scale_mlp)
         )
         branch_grad = (gate_att * middle_grad).astype(B16)
-        grads_bf[2] = dot(branch_grad, w_proj[...], NT).astype(B16)
-        qkvp[3] = dot(mixed[...], branch_grad, TN)
+        mixed_grad[...] = dot(branch_grad, w_proj[...], NT).astype(B16)
+        qkvp[3] = dot(mixed_t[...], branch_grad, MM)
         yield
         mod_own[5:6, :] = col_sum(gradient * mlp_out)
         mod_own[4:5, :] = col_sum(second_grad * second_normed)
@@ -750,8 +752,8 @@
         for pair in range(head_pairs):
             lanes = slice(pair * 128, (pair + 1) * 128)
             v_lanes = slice(width + pair * 128, width + (pair + 1) * 128)
-            keys, values, queries = kv_all[:, lanes], kv_all[:, v_lanes], q_all[:, lanes]
-            out_grad = grads_bf[2, :, lanes].astype(F32)
+            values, queries = kv_all[:, v_lanes], q_all[:, lanes]
+            out_grad = mixed_grad[:, lanes].astype(F32)
             parts = []
             key_grad = jnp.zeros((2 * own, 128), F32)
             value_grad = jnp.zeros((2 * own, 128), F32)
@@ -767,15 +769,17 @@
                 score_grad = (wide_weights * (weight_grad - row_sum)).astype(B16)
                 value_grad = value_grad + dot(weights, masked_grad, MM)
                 key_grad = key_grad + dot(score_grad, queries * halves[half], MM)
-                query_grad = dot(keys, score_grad, TN)
+                query_grad = dot(keys_t[lanes, :], score_grad, MM)
                 parts.append(query_grad[half * HEAD_DIM : (half + 1) * HEAD_DIM])
+                if half == 0:
+                    yield
             query_grad = jnp.concatenate(parts, axis=0).T * inv_root
             dq[:, lanes] = query_grad.astype(B16)
             dkv[:, lanes] = key_grad.astype(B16)
             dkv[:, v_lanes] = value_grad.astype(B16)
-            qkvp[pair, :, :128] = dot(entry[:own, :], dq[:, lanes], TN)
-            qkvp[pair, :, 128:256] = dot(entry[...], dkv[:, lanes], TN)
-            qkvp[pair, :, 256:] = dot(entry[...], dkv[:, v_lanes], TN)
+            qkvp[pair, :, :128] = dot(entry_t[:, :own], dq[:, lanes], MM)
+            pair_grads = jnp.concatenate([key_grad, value_grad], axis=1).astype(B16)
+            qkvp[pair, :, 128:] = dot(entry_t[...], pair_grads, MM)
             if pair == 0:
                 core_out[2, :width, :] = qkvp[3 * (1 - core)].astype(B16)
                 core_start(2, 0, width)
@@ -969,10 +973,14 @@
         pltpu.VMEM((own, width), B16),
         pltpu.VMEM((own, width), F32),
         pltpu.VMEM((own, width), F32),
-        pltpu.VMEM((blocks, own, width), B16),
+        pltpu.VMEM((blocks, width, own), B16),
         pltpu.VMEM((blocks, own, width), F32),
         pltpu.VMEM((blocks, own, width), B16),
-        pltpu.VMEM((3, own, width), B16),
+        pltpu.VMEM((own, width), B16),
+        pltpu.VMEM((width, 2 * own), B16),
+        pltpu.VMEM((width, own), B16),
+        pltpu.VMEM((width, own), B16),
+        pltpu.VMEM((width, 2 * own), B16),
         pltpu.VMEM((2, items, span, width), B16),
         pltpu.VMEM((own, width), F32),
         pltpu.VMEM((own, width), F32),

time: 65.9 us -> 64.2 us (0.974)
  Pallas kernels: 64.9 us -> 63.3 us
    pallas_call x1, Pallas kernels: 60.3 us -> 58.6 us  [fused(): pl.pallas_call(fused_kernel, out_shape=(pltpu.VMEM(block_in.shape, B16),...]
where the time goes in v4:
time: 64.2 us; the launch traced here: 64.1 us
  Pallas kernels  63.3 us (99%)
  between operations  0.81 us (1%)
    pallas_call x1, Pallas kernels, fused(): pl.pallas_call(fused_kernel, out_shape=(pltpu.VMEM(block_in.shape, B16),...  58.6 us
    pallas_call x1, Pallas kernels, widen(): pl.pallas_call(widen_kernel, out_shape=tuple((jax.ShapeDtypeStruct(shape,...  4.65 us

profile of v4, /device:TPU:0, one launch (start us, length us, event | category | flops | bytes accessed | tf_op | source)
XLA Modules:
  0.0 64.1 jit_solution(2860185979756341425)
XLA Ops:
  0.6 58.6 %fused_block.1 = (bf16[4,64,384]{2,1,0:T(8,128)(2,1)S(1)}, bf16[4,64,384]{2,1,0:T(8,128)(2,1)S(1)}, bf16[3,1536,384]{2,1,0:T(8,128)(2,1)S(1)}, f32[16,8,384]{2,1,0:T(8,128)S(1)}) custom-call(s32[4]{0:T(128)} %lengths_in.1, bf16[4,64,384]{2,1,0:T(8,128)(2,1)} %block_in.1, bf16[4,64,384]{2,1,0:T(8,128)(2,1)} %cotangent.1, bf16[4,384]{1,0:T(4,128)(2,1)} %lead_embed_in.1, ...), custom_call_target="tpu_custom_call" | custom-call | tf_op jit(solution)/shard_map/fused_block/pallas_call | solution.py:1002
  59.2 4.7 %widen.1 = (f32[4,64,384]{2,1,0:T(8,128)}, f32[4,64,384]{2,1,0:T(8,128)}, f32[384,2304]{1,0:T(8,128)}, f32[2304]{0:T(1024)}, f32[384,1152]{1,0:T(8,128)}, /*inde...) custom-call(bf16[4,64,384]{2,1,0:T(8,128)(2,1)S(1)} %get-tuple-element.12.block_16, ...), custom_call_target="tpu_custom_call" | custom-call | tf_op jit(solution)/shard_map/widen/pallas_call | solution.py:929

commit v5 on v4

--- a/solution.py
+++ b/solution.py
@@ -420,8 +420,8 @@
         pltpu.make_async_copy(area, area, sem).wait()
 
     barrier = pltpu.get_barrier_semaphore()
-    greet = [core_peer, x_peer, y_peer, xy_peer]
-    greet += [at(y, x, (z + step) % items, core) for step in range(1, items)]
+    greet = [at(y, x, (z + step) % items, core) for step in (2, 3, 1)]
+    greet += [xy_peer, x_peer, y_peer, core_peer]
     for device in greet:
         pl.semaphore_signal(barrier, inc=1, device_id=device, device_id_type=MESH)
     loads = [

time: 64.2 us -> 64.2 us (level)
  no operation moved by 1% of the time
where the time goes in v5:
time: 64.2 us; the launch traced here: 64.1 us
  Pallas kernels  63.3 us (99%)
  between operations  0.81 us (1%)
    pallas_call x1, Pallas kernels, fused(): pl.pallas_call(fused_kernel, out_shape=(pltpu.VMEM(block_in.shape, B16),...  58.6 us
    pallas_call x1, Pallas kernels, widen(): pl.pallas_call(widen_kernel, out_shape=tuple((jax.ShapeDtypeStruct(shape,...  4.65 us

profile of v5, /device:TPU:0, one launch (start us, length us, event | category | flops | bytes accessed | tf_op | source)
XLA Modules:
  0.0 64.1 jit_solution(11256877067864965568)
XLA Ops:
  0.6 58.6 %fused_block.1 = (bf16[4,64,384]{2,1,0:T(8,128)(2,1)S(1)}, bf16[4,64,384]{2,1,0:T(8,128)(2,1)S(1)}, bf16[3,1536,384]{2,1,0:T(8,128)(2,1)S(1)}, f32[16,8,384]{2,1,0:T(8,128)S(1)}) custom-call(s32[4]{0:T(128)} %lengths_in.1, bf16[4,64,384]{2,1,0:T(8,128)(2,1)} %block_in.1, bf16[4,64,384]{2,1,0:T(8,128)(2,1)} %cotangent.1, bf16[4,384]{1,0:T(4,128)(2,1)} %lead_embed_in.1, ...), custom_call_target="tpu_custom_call" | custom-call | tf_op jit(solution)/shard_map/fused_block/pallas_call | solution.py:1002
  59.3 4.6 %widen.1 = (f32[4,64,384]{2,1,0:T(8,128)}, f32[4,64,384]{2,1,0:T(8,128)}, f32[384,2304]{1,0:T(8,128)}, f32[2304]{0:T(1024)}, f32[384,1152]{1,0:T(8,128)}, /*inde...) custom-call(bf16[4,64,384]{2,1,0:T(8,128)(2,1)S(1)} %get-tuple-element.12.block_16, ...), custom_call_target="tpu_custom_call" | custom-call | tf_op jit(solution)/shard_map/widen/pallas_call | solution.py:929
